TPU v7x, 512 devices: a whole 4x4x16 slice. The times are simulated.
512 devices in a mesh: pair: 32 (over z_lo, y), vtile: 8 (over x, core), irrep: 2 (over z_hi).
Axes of the slice: x: 4, y: 4, z: 16 (z_hi: 2, z_lo: 8; z = z_hi * 8 + z_lo), core: 2. Of those that a mesh axis runs over, the one named last changes fastest.
Arguments:
- amplitudes: bfloat16 [160, 8, 7744], P('pair'), may hold values from -4 to 4
- slabs: bfloat16 [32, 8, 2, 88, 7744], P('pair', 'vtile', 'irrep'), may hold values from -1.5 to 1.5
- couplings: bfloat16 [2, 30, 30, 176], P(None, None, None, 'irrep'), may hold values from -6 to 6
- occ_energy: float32 [30], replicated, may hold values from -2 to -0.3
- vir_energy: float32 [8, 88], replicated, may hold values from 0.2 to 4
- occ_irrep: int32 [30], replicated, may hold values from 0 to 7
- pair_i: int32 [160], P('pair'), may hold values from 0 to 29, as said below
- pair_j: int32 [160], P('pair'), may hold values from 0 to 29, as said below
- window_k: int32 [2], replicated, may hold values from 0 to 29
- owner: int32 [2], replicated, may hold values from 0 to 31
Outputs:
- resid_part: float32 [160, 8, 7744], P('pair', 'vtile', 'irrep')
Inputs may be any that keep to these rules, and one draw needn't show every extreme that they name: Pairs come in groups of 16 that share pair_i; groups have different pair_i. Within a group of pairs sharing pair_i, pair_j values are distinct.
All inputs are finite; a program needn't handle non-finite values.
Results may differ from a plain program's by a relative error of at most 0.0003.
Values may be sent and summed in bfloat16 or wider, within the bound.
A program may use at most 64 MiB of HBM per device.

v0:
```python
import jax
import jax.numpy as jnp
from jax import lax
from jax.sharding import PartitionSpec as P

K_WIN = 2


def spread(shard, axis, root):
    mine = lax.axis_index(axis) == root
    return lax.psum(jnp.where(mine, shard, jnp.zeros_like(shard)), axis)


def on_device(
    amplitudes, slabs, couplings, occ_energy, vir_energy, occ_irrep, pair_i, pair_j, window_k, owner
):
    tile_blocks = slabs.shape[1]
    block_size = slabs.shape[3]
    block_area = block_size * block_size
    local_pairs = amplitudes.shape[0]
    tile_index = lax.axis_index("vtile")
    gamma_irrep = lax.axis_index("irrep")
    beta_irreps = tile_index * tile_blocks + jnp.arange(tile_blocks, dtype=jnp.int32)
    pair_sym = jnp.bitwise_xor(occ_irrep[pair_i], occ_irrep[pair_j])
    send_index = jnp.bitwise_xor(beta_irreps[None, :], pair_sym[:, None])
    outgoing = jnp.take_along_axis(amplitudes, send_index[:, :, None], axis=1)
    local_slab = slabs[0, :, 0]
    gamma_energy = jnp.take(vir_energy, gamma_irrep, axis=0)
    beta_energy = vir_energy[beta_irreps]
    occ_keep = jnp.bitwise_xor(occ_irrep, gamma_irrep)

    def pair_term(amp_pair, occ_i, occ_j, hole_part, slab_data, k_irrep, k_energy):
        pair_irrep = jnp.bitwise_xor(occ_irrep[occ_i], occ_irrep[occ_j])
        alpha_irrep = jnp.bitwise_xor(
            jnp.bitwise_xor(pair_irrep, k_irrep), jnp.bitwise_xor(beta_irreps, gamma_irrep)
        )
        amp_sel = amp_pair[alpha_irrep].reshape(tile_blocks, block_size, block_size)
        particle = jnp.einsum(
            "mad,mdx->max", amp_sel, slab_data, preferred_element_type=jnp.float32
        )
        energy_a = vir_energy[alpha_irrep]
        base = occ_energy[occ_i] + occ_energy[occ_j] + k_energy
        denominator = (
            energy_a[:, :, None, None]
            + beta_energy[:, None, :, None]
            + gamma_energy[None, None, None, :]
            - base
        )
        triples = (
            (particle - hole_part) / denominator.reshape(tile_blocks, block_size, block_area)
        ).astype(jnp.bfloat16)
        contrib = jnp.einsum("max,mdx->mad", triples, slab_data, preferred_element_type=jnp.float32)
        return (
            jnp.zeros((8, block_area), jnp.float32)
            .at[alpha_irrep]
            .add(contrib.reshape(tile_blocks, block_area))
        )

    def coupling_rows(window, occ_j, k_irrep):
        y_column = jnp.take(couplings[window], occ_j, axis=1)
        keep_mask = jnp.bitwise_xor(occ_keep, jnp.bitwise_xor(occ_irrep[occ_j], k_irrep)) == 0
        return y_column.astype(jnp.float32) * keep_mask[:, None].astype(jnp.float32)

    hole_amp, all_first, all_second = (
        lax.all_gather(outgoing, "pair", axis=0, tiled=True),
        lax.all_gather(pair_i, "pair", axis=0, tiled=True),
        lax.all_gather(pair_j, "pair", axis=0, tiled=True),
    )
    accumulated = jnp.zeros((local_pairs, 8, block_area), jnp.float32)
    for window in range(K_WIN):
        slab_data = spread(local_slab, "pair", owner[window])
        k_index = window_k[window]
        k_irrep = occ_irrep[k_index]
        k_energy = occ_energy[k_index]

        def gathered_step(packed):
            amp_pair, occ_i, occ_j = packed
            coef_rows = coupling_rows(window, occ_j, k_irrep)
            members = jnp.argsort(
                jnp.where(all_first == occ_i, 0, 1).astype(jnp.int32), stable=True
            )[:16]
            member_amp = jnp.take(hole_amp, members, axis=0)
            coupling = jnp.take(coef_rows, jnp.take(all_second, members), axis=0).astype(
                jnp.bfloat16
            )
            hole_part = jnp.einsum(
                "qmx,qc->mxc", member_amp, coupling, preferred_element_type=jnp.float32
            )
            hole_part = hole_part.reshape(tile_blocks, block_size, block_area)
            return pair_term(amp_pair, occ_i, occ_j, hole_part, slab_data, k_irrep, k_energy)

        contrib_all = lax.map(gathered_step, (amplitudes, pair_i, pair_j))
        accumulated = accumulated + contrib_all
    summed = lax.psum(accumulated, ("vtile", "irrep"))
    irrep_count = lax.axis_size("irrep")
    share = block_area // irrep_count
    summed = lax.dynamic_slice_in_dim(summed, tile_index * tile_blocks, tile_blocks, 1)
    return lax.dynamic_slice_in_dim(summed, gamma_irrep * share, share, 2)


def solution(mesh):
    placed = (
        P("pair", None, None),
        P("pair", "vtile", "irrep", None, None),
        P(None, None, None, "irrep"),
        P(),
        P(),
        P(),
        P("pair"),
        P("pair"),
        P(),
        P(),
    )
    return jax.shard_map(
        on_device,
        mesh=mesh,
        in_specs=placed,
        out_specs=P("pair", "vtile", "irrep"),
        check_vma=False,
    )
```

profile of v0, /device:TPU:1, one launch (start us, length us, event | category | flops | bytes accessed | tf_op | source)
XLA Modules:
  0.0 1475.7 jit_solution(15392690498149942360)
XLA Ops:
  24.3 23.3 %all-reduce.2 = (s32[160]{0:T(256)S(1)}, s32[160]{0:T(256)S(1)}) all-reduce(s32[160]{0:T(256)S(1)} %dynamic-update-slice.19, s32[160]{0:T(256)S(1)} %dynamic-update-slice.20), channel_id=1, replica_groups=mesh['pair'=32,'vtile'=8,'irrep'=2] {'pair'}, use_global_device_ids=true, to_apply=%add | all-reduce | flops 320 | bytes 2560
  47.6 181.2 %all-gather.2.cloned.1.call-done = bf16[160,1,7744]{2,1,0:T(2,128)(2,1)} async-done(((bf16[5,1,7744]{2,1,0:T(2,128)(2,1)}), bf16[160,1,7744]{2,1,0:T(2,128)(2,1)}) %all-gather.2.cloned.1.call-update) | async-done | bytes 2478096 | tf_op jit(solution)/shard_map/all_gather | solution.py:65
  231.5 458.8 %all-reduce.9.cloned.1.call-done = (bf16[1,88,7744]{2,1,0:T(8,128)(2,1)}, bf16[1,88,7744]{2,1,0:T(8,128)(2,1)}) async-done(((bf16[1,88,7744]{2,1,0:T(8,128)(2,1)}, bf16[1,88,7744]{2,1,0:T(8,128)(2,1)}), (bf16[1,88,7744]{2,1,0:T(8,128)(2,1)}, bf16[1,88,7744]{2,1,0:T(8,128)(2,1)})) %all-reduce.9.cloned.1.call-update) | async-done | bytes 2725904 | tf_op jit(solution)/shard_map/psum | solution.py:11
  691.5 204.7 %while.34 = (s32[]{:T(128)}, f32[5,8,7744]{2,1,0:T(8,128)}, s32[5]{0:T(128)S(1)}, s32[30]{0:T(128)S(1)}, s32[5]{0:T(128)S(1)}, /*index=5*/s32[]{:T(128)}, s32[1]...) while((s32[]{:T(128)}, f32[5,8,7744]{2,1,0:T(8,128)}, ...), condition=%wide.region_9.14_spmd, body=%wide.region_6.13_spmd.sunk | while | flops 265247984 | bytes 25429668 | solution.py:92
  707.0 5.0 reshape.780
  716.4 5.1 add.410
  725.8 5.0 fusion.92
  747.9 5.0 reshape.780
  757.4 5.1 add.410
  788.8 5.0 reshape.780
  798.3 5.1 add.410
  829.8 5.0 reshape.780
  839.3 5.1 add.410
  870.7 5.0 reshape.780
  880.2 5.1 add.410
  897.3 206.2 %while.33 = (s32[]{:T(128)}, f32[5,8,7744]{2,1,0:T(8,128)}, s32[5]{0:T(128)S(1)}, s32[30]{0:T(128)S(1)}, s32[5]{0:T(128)S(1)}, /*index=5*/s32[]{:T(128)}, s32[1]...) while((s32[]{:T(128)}, f32[5,8,7744]{2,1,0:T(8,128)}, ...), condition=%wide.region_4.9_spmd, body=%wide.region_1.8_spmd.sunk | while | flops 265247984 | bytes 25429668 | solution.py:92
  912.9 5.0 reshape.772
  922.4 5.1 add.394
  931.9 5.1 fusion.83
  954.1 5.0 reshape.772
  963.7 5.1 add.394
  973.1 5.1 fusion.83
  995.4 5.0 reshape.772
  1004.9 5.1 add.394
  1014.4 5.1 fusion.83
  1036.6 5.0 reshape.772
  1046.2 5.1 add.394
  1055.6 5.1 fusion.83
  1077.9 5.0 reshape.772
  1087.4 5.1 add.394
  1096.8 5.1 fusion.83
  1106.4 360.9 %all-reduce.7.cloned.1.call-done = f32[5,8,7744]{2,1,0:T(8,128)} async-done(((f32[5,8,7744]{2,1,0:T(8,128)}), f32[5,8,7744]{2,1,0:T(8,128)}) %all-reduce.7.cloned.1.call-update) | async-done | bytes 1239056 | tf_op jit(solution)/shard_map/psum | solution.py:94
  (363 shorter events, 213.4 us)
Async XLA Ops:
  6.5 3.6 copy-start.1
  6.5 222.2 %all-gather.2.cloned.1.call-start = ((), (), s32[]{:S(2)}) async-start(), calls=%async_computation | async-start | bytes 5153280 | tf_op jit(solution)/shard_map/all_gather | solution.py:65
  7.3 4.7 copy-start.6
  7.3 6.5 copy-start.2
  12.0 678.3 %all-reduce.9.cloned.1.call-start = ((), (), s32[]{:S(2)}) async-start(), calls=%async_computation.2 | async-start | bytes 5496832 | tf_op jit(solution)/shard_map/psum | solution.py:11
  15.6 0.7 copy-start.7
  15.6 5.6 copy-start.9
  15.6 5.9 copy-start.8
  15.6 6.1 copy-start.3
  15.6 7.5 copy-start
  15.6 8.1 copy-start.4
  15.6 32.0 %copy-start.10 = (f32[8,88]{1,0:T(8,128)S(1)}, f32[8,88]{1,0:T(8,128)}, u32[]{:S(2)}) copy-start(f32[8,88]{1,0:T(8,128)} %param.30) | copy-start | bytes 8452
  15.6 1451.6 %all-reduce.7.cloned.1.call-start = ((), (), s32[]{:S(2)}) async-start(), calls=%async_computation.1 | async-start | bytes 2498560 | tf_op jit(solution)/shard_map/psum | solution.py:94
  47.6 643.9 %copy-start.5 = (s32[2]{0:T(128)S(1)}, s32[2]{0:T(128)}, u32[]{:S(2)}) copy-start(s32[2]{0:T(128)} %constant.209.clone.1) | copy-start | bytes 28
Sparse Core Ops, SparseCore 0:
  12.1 216.6 all-gather.1
  231.8 458.4 all-reduce.8
  1106.5 360.7 all-reduce.6
where the time goes:
time: 1490 us; the launch traced here: 1480 us
  waiting for transfers between devices  1000 us (67%)
  local copies, waits for them, and re-layouts  214 us (14%)
  loops' own time  88.4 us (6%)
  matrix products  76.7 us (5%)
  other arithmetic  53.1 us (4%)
  blocking collectives  23.3 us (2%)
  between operations  18.9 us (1%)
    psum x1, waiting for transfers between devices, spread(): return lax.psum(jnp.where(mine, shard, jnp.zeros_like(shard)), axis)  459 us
    psum x1, waiting for transfers between devices, on_device(): summed = lax.psum(accumulated, ('vtile', 'irrep'))  361 us
    all_gather x1, waiting for transfers between devices, on_device(): lax.all_gather(outgoing, 'pair', axis=0, tiled=True)  181 us
    another operation x2, loops' own time, on_device(): contrib_all = lax.map(gathered_step, (amplitudes, pair_i, pair_j))  88.4 us
    add x50, local copies, waits for them, and re-layouts, pair_term(): energy_a[:, :, None, None] + beta_energy[:, None, :, None]  77.4 us
    reshape x10, local copies, waits for them, and re-layouts, gathered_step(): hole_part = hole_part.reshape(tile_blocks, block_size, block_area)  50 us
    dot_general x10, matrix products, pair_term(): jnp.einsum('max,mdx->mad', triples, slab_data, preferred_element_type=jnp...  50 us
    sort x10, other arithmetic, gathered_step(): jnp.argsort(jnp.where(all_first == occ_i, 0, 1).astype(jnp.int32), stable...  31.7 us
  transfers between devices with their start and end apart: 3, of which 3 were waited for; matrix products, arithmetic and copies ran while one was open for 1% of the time, Pallas kernels for 0%

commit v1 on v0

v1 whole, which is shorter than its diff:
```python
import jax
import jax.numpy as jnp
from jax import lax
from jax.experimental import pallas as pl
from jax.experimental.pallas import tpu as pltpu
from jax.sharding import PartitionSpec as P

MESH = pl.DeviceIdType.MESH
YS, ZS, XS = 4, 8, 4
BLK = 88
PER = 5
NW = 2
BCH = BLK // YS
CHL = 2048
LAST = 7808
NCH = 8
CW = CHL // NCH
SKEW = 2
PACK = 896
OUTL = 512
ZSTEPS = (1, 2, 3, 4, -1, -2, -3)
VM = pl.BlockSpec(memory_space=pltpu.VMEM)
SM = pl.BlockSpec(memory_space=pltpu.SMEM)


def where_am_i():
    pair, vtile, irrep = lax.axis_index("pair"), lax.axis_index("vtile"), lax.axis_index("irrep")
    return pair, vtile, irrep, lax.rem(pair, YS), pair // YS


def spread_kernel(
    owner_ref, slab_ref, part_ref, hole_ref,
    vsel_ref, pall_ref, hall_ref,
    ybuf, frecv, brecv, fsend, bsend,
    ys_sem, yr_sem, hs_sem, hr_sem, ps_sem, pr_sem,
    fs_sem, fr_sem, bs_sem, br_sem, zs_sem, zr_sem, local_sem,
):
    pair, vtile, irrep, y, z = where_am_i()
    zg = irrep * ZS + z

    def at_y(k):
        ty = lax.rem(y + k + YS, YS)
        return ty, (z * YS + ty, vtile, irrep)

    def at_z(step):
        tz = lax.rem(zg + step + 2 * ZS, 2 * ZS)
        return (lax.rem(tz, ZS) * YS + y, vtile, tz // ZS)

    barrier = pltpu.get_barrier_semaphore()
    for k in (1, 2, 3):
        pl.semaphore_signal(barrier, inc=1, device_id=at_y(k)[1], device_id_type=MESH)
    for step in (1, 2, 3, 4, -1, -2, -3, -4):
        pl.semaphore_signal(barrier, inc=1, device_id=at_z(step), device_id_type=MESH)
    pl.semaphore_wait(barrier, 11)

    def hole_copy(k):
        ty, target = at_y(k)
        return pltpu.make_async_remote_copy(
            src_ref=hole_ref.at[ty], dst_ref=hall_ref.at[z, y],
            send_sem=hs_sem.at[k - 1], recv_sem=hr_sem.at[k - 1],
            device_id=target, device_id_type=MESH)

    def part_copy(k):
        _, target = at_y(k)
        return pltpu.make_async_remote_copy(
            src_ref=part_ref, dst_ref=pall_ref.at[y],
            send_sem=ps_sem.at[k - 1], recv_sem=pr_sem.at[k - 1],
            device_id=target, device_id_type=MESH)

    def slab_copy(k, n):
        ty, target = at_y(k)
        start = pl.multiple_of(ty * 1920 + n * CW, 128)
        return pltpu.make_async_remote_copy(
            src_ref=slab_ref.at[:, pl.ds(start, CW)],
            dst_ref=ybuf.at[y, :, pl.ds(pl.multiple_of(n * CW, CW), CW)],
            send_sem=ys_sem.at[k - 1, n], recv_sem=yr_sem.at[k - 1, n],
            device_id=target, device_id_type=MESH)

    def ring_copy(index):
        step = ZSTEPS[index]
        return pltpu.make_async_remote_copy(
            src_ref=hall_ref.at[z], dst_ref=hall_ref.at[z],
            send_sem=zs_sem.at[index], recv_sem=zr_sem.at[index],
            device_id=at_z(step), device_id_type=MESH)

    def chain_copy(forward, n):
        lanes = pl.ds(pl.multiple_of(n * CW, CW), CW)
        src, dst = (fsend, frecv) if forward else (bsend, brecv)
        send, recv = (fs_sem, fr_sem) if forward else (bs_sem, br_sem)
        tz = jnp.minimum(z + 1, ZS - 1) if forward else jnp.maximum(z - 1, 0)
        return pltpu.make_async_remote_copy(
            src_ref=src.at[:, :, lanes], dst_ref=dst.at[:, :, lanes],
            send_sem=send.at[n], recv_sem=recv.at[n],
            device_id=(tz * YS + y, vtile, irrep), device_id_type=MESH)

    for k in (1, 3, 2):
        hole_copy(k).start()

    def send_chunk(n, _):
        for k in (1, 3, 2):
            slab_copy(k, n).start()
        return 0

    lax.fori_loop(0, NCH, send_chunk, 0)
    for k in (1, 3, 2):
        part_copy(k).start()

    own_slab = pltpu.make_async_copy(
        slab_ref.at[:, pl.ds(pl.multiple_of(y * 1920, 128), CHL)], ybuf.at[y], local_sem.at[0])
    own_part = pltpu.make_async_copy(part_ref, pall_ref.at[y], local_sem.at[1])
    own_hole = pltpu.make_async_copy(hole_ref.at[y], hall_ref.at[z, y], local_sem.at[2])
    for copy in (own_slab, own_part, own_hole):
        copy.start()
    own_hole.wait()
    for k in (1, 2, 3):
        hole_copy(k).wait_recv()
    for index in (0, 4, 1, 5, 2, 6, 3):
        ring_copy(index).start()
    own_slab.wait()
    own_part.wait()

    root_y = [lax.rem(owner_ref[w], YS) for w in range(NW)]
    root_z = [owner_ref[w] // YS for w in range(NW)]

    def wait_y(n):
        for k in (1, 2, 3):
            slab_copy(k, n).wait_recv()

    def candidate(w, lanes):
        value = ybuf[0, :, lanes]
        for source in range(1, YS):
            value = jnp.where(root_y[w] == source, ybuf[source, :, lanes], value)
        return value

    def chain_event(forward, n):
        lanes = pl.ds(pl.multiple_of(n * CW, CW), CW)
        src, dst = (fsend, frecv) if forward else (bsend, brecv)
        first_here = z <= 3 if forward else z >= 4
        start, end = (z == 0, z == ZS - 1) if forward else (z == ZS - 1, z == 0)

        @pl.when(first_here)
        def _():
            wait_y(n)

        mine = [candidate(w, lanes) for w in range(NW)]

        @pl.when(start)
        def _():
            for w in range(NW):
                dst[w, :, lanes] = mine[w]

        @pl.when(jnp.logical_not(start))
        def _():
            chain_copy(forward, n).wait_recv()

        if forward:
            for w in range(NW):
                vsel_ref[w, :, lanes] = mine[w]

        @pl.when(jnp.logical_not(end))
        def _():
            for w in range(NW):
                src[w, :, lanes] = jnp.where(root_z[w] == z, mine[w], dst[w, :, lanes])
            chain_copy(forward, n).start()

    def chain_step(t, _):
        nf = t - SKEW * z
        nb = t - SKEW * (ZS - 1 - z)

        @pl.when(jnp.logical_and(nf >= 0, nf < NCH))
        def _():
            chain_event(True, nf)

        @pl.when(jnp.logical_and(nb >= 0, nb < NCH))
        def _():
            chain_event(False, nb)

        return 0

    lax.fori_loop(0, NCH + SKEW * (ZS - 1), chain_step, 0)

    def settle(n, _):
        lanes = pl.ds(pl.multiple_of(n * CW, CW), CW)
        for w in range(NW):
            other = jnp.where(root_z[w] < z, frecv[w, :, lanes], brecv[w, :, lanes])
            vsel_ref[w, :, lanes] = jnp.where(root_z[w] == z, vsel_ref[w, :, lanes], other)
        return 0

    lax.fori_loop(0, NCH, settle, 0)

    for k in (1, 2, 3):
        part_copy(k).wait_recv()
    for index in range(len(ZSTEPS)):
        tz = lax.rem(zg - ZSTEPS[index] + 2 * ZS, 2 * ZS)
        pltpu.make_async_remote_copy(
            src_ref=hall_ref.at[z], dst_ref=hall_ref.at[lax.rem(tz, ZS)],
            send_sem=zs_sem.at[index], recv_sem=zr_sem.at[index],
            device_id=at_z(ZSTEPS[index]), device_id_type=MESH).wait_recv()

    def sent(n, _):
        for k in (1, 2, 3):
            slab_copy(k, n).wait_send()

        @pl.when(z < ZS - 1)
        def _():
            chain_copy(True, n).wait_send()

        @pl.when(z > 0)
        def _():
            chain_copy(False, n).wait_send()

        return 0

    lax.fori_loop(0, NCH, sent, 0)
    for k in (1, 2, 3):
        hole_copy(k).wait_send()
        part_copy(k).wait_send()
    for index in range(len(ZSTEPS)):
        ring_copy(index).wait_send()


def window_of(offset, width):
    base = offset // 128 * 128
    return base, 128 if offset - base + width <= 128 else 256


def cut(value, offset):
    moved = pltpu.roll(value, value.shape[1] - offset, 1) if offset else value
    moved = moved[:, :128]
    lane = lax.broadcasted_iota(jnp.int32, moved.shape, 1)
    return jnp.where(lane < BLK, moved, 0.0)


def work_kernel(
    place_ref, first_ref, second_ref,
    hall_ref, vsel_ref, pall_ref, coup_ref, ea_ref, ebc_ref,
    out_ref,
    wide, left, vshift, vtile_ref, amp_ref, weight, holes, trip, column,
):
    y = place_ref[0]
    wide[...] = hall_ref[...].astype(jnp.float32)
    for k in range(16):
        tile = wide[pl.ds(k, 160, stride=16), :]
        left[128 * k:128 * k + 128, :] = tile.T.astype(jnp.bfloat16)
    table = wide[pl.ds(15, 160, stride=16), :]
    group, member = table[:, 16:17], table[:, 17:18]
    slot = lax.broadcasted_iota(jnp.int32, (160, 32), 1).astype(jnp.float32)
    for p in range(YS * PER):
        here = jnp.logical_and(member == slot, group == first_ref[p].astype(jnp.float32))
        pick = here.astype(jnp.float32).astype(jnp.bfloat16)
        both = jnp.dot(pick, coup_ref[second_ref[p]], preferred_element_type=jnp.float32)
        for w in range(NW):
            weight[w, :, 128 * p:128 * p + 128] = both[:, 128 * w:128 * w + 128].astype(jnp.bfloat16)

    for w in range(NW):
        for shift in range(YS):
            @pl.when(y == shift)
            def _():
                value = vsel_ref[w].astype(jnp.float32)
                vshift[...] = pltpu.roll(value, CHL - 16 * shift, 1) if shift else value
        for b in range(BCH):
            base, width = window_of(BLK * b, BLK)
            vtile_ref[:, 128 * b:128 * b + 128] = cut(
                vshift[:, base:base + width], BLK * b - base).astype(jnp.bfloat16)
        for source in range(YS):
            parts = []
            for p in range(PER):
                offset = BLK * (w * PER + p)
                base, width = window_of(offset, BLK)
                parts.append(cut(pall_ref[source, :, base:base + width].astype(jnp.float32), offset - base))
            amp_ref[source] = jnp.concatenate(parts, axis=0).astype(jnp.bfloat16)

        def hole_step(t, _):
            lanes = pl.ds(pl.multiple_of(t * 256, 256), 256)
            holes[:, lanes] = jnp.dot(
                left[:BCH * BLK, :], weight[w, :, lanes], preferred_element_type=jnp.float32)
            return 0

        lax.fori_loop(0, YS * PER // 2, hole_step, 0)

        def source_step(source, _):
            column[...] = jnp.broadcast_to(ea_ref[w * YS + source], (PER * BLK, 128))

            def tile_step(t, _):
                lanes = pl.ds(pl.multiple_of(t * 256, 256), 256)
                particle = jnp.dot(
                    amp_ref[source, :, :BLK], vtile_ref[:, lanes], preferred_element_type=jnp.float32)
                for half in range(2):
                    rows = pl.ds(pl.multiple_of((2 * t + half) * BLK, 8), BLK)
                    hole = jnp.concatenate([
                        holes[rows, pl.ds(pl.multiple_of((source * PER + p) * 128, 128), 128)]
                        for p in range(PER)], axis=0)
                    denominator = column[...] + ebc_ref[2 * t + half]
                    guess = pl.reciprocal(denominator, approx=True)
                    guess = guess * (2.0 - denominator * guess)
                    guess = guess * (2.0 - denominator * guess)
                    value = (particle[:, 128 * half:128 * half + 128] - hole) * guess
                    trip[source, :, pl.ds(pl.multiple_of(t * 256 + 128 * half, 128), 128)] = value.astype(jnp.bfloat16)
                return 0

            lax.fori_loop(0, BCH // 2, tile_step, 0)
            return 0

        lax.fori_loop(0, YS, source_step, 0)
        for source in range(YS):
            contrib = lax.dot_general(
                trip[source], vtile_ref[...], (((1,), (1,)), ((), ())), preferred_element_type=jnp.float32)
            for p in range(PER):
                offset = BLK * (w * PER + p)
                out_ref[source, :, offset:offset + BLK] = contrib[BLK * p:BLK * p + BLK]
    for source in range(YS):
        out_ref[source, :, 880:PACK] = jnp.zeros((BLK, PACK - 880), jnp.float32)


def sum_kernel(
    code_ref, c_ref, out_ref,
    ybuf, slots, cbuf, merged, xbuf, total, zbuf,
    ys_sem, yr_sem, cs_sem, cr_sem, xs_sem, xr_sem, zs_sem, zr_sem,
):
    pair, vtile, irrep, y, z = where_am_i()
    x, core = vtile // 2, lax.rem(vtile, 2)

    def at_y(k):
        ty = lax.rem(y + k, YS)
        return ty, (z * YS + ty, vtile, irrep)

    def at_x(k):
        tx = lax.rem(x + k, XS)
        return tx, (pair, tx * 2 + core, irrep)

    at_core = (pair, x * 2 + 1 - core, irrep)
    at_irrep = (pair, vtile, 1 - irrep)
    barrier = pltpu.get_barrier_semaphore()
    for k in (1, 2, 3):
        pl.semaphore_signal(barrier, inc=1, device_id=at_y(k)[1], device_id_type=MESH)
        pl.semaphore_signal(barrier, inc=1, device_id=at_x(k)[1], device_id_type=MESH)
    pl.semaphore_signal(barrier, inc=1, device_id=at_core, device_id_type=MESH)
    pl.semaphore_signal(barrier, inc=1, device_id=at_irrep, device_id_type=MESH)
    pl.semaphore_wait(barrier, 8)

    ycopies = []
    for k in (1, 3, 2):
        ty, target = at_y(k)
        ycopies.append(pltpu.make_async_remote_copy(
            src_ref=c_ref.at[ty], dst_ref=ybuf.at[k - 1],
            send_sem=ys_sem.at[k - 1], recv_sem=yr_sem.at[k - 1],
            device_id=target, device_id_type=MESH))
    for copy in ycopies:
        copy.start()
    for copy in ycopies:
        copy.wait()
    summed = c_ref[y] + ybuf[0] + ybuf[1] + ybuf[2]
    windows = [summed[:, :OUTL], pltpu.roll(summed, PACK - 440, 1)[:, :OUTL]]
    codes = [code_ref[w:w + 1, :] for w in range(NW)]
    for target in range(2 * XS):
        slots[target % 2, target // 2] = sum(
            jnp.where(codes[w] == target, windows[w], 0.0) for w in range(NW))
    ccopy = pltpu.make_async_remote_copy(
        src_ref=slots.at[1 - core], dst_ref=cbuf,
        send_sem=cs_sem, recv_sem=cr_sem, device_id=at_core, device_id_type=MESH)
    ccopy.start()
    ccopy.wait()
    for tx in range(XS):
        merged[tx] = slots[core, tx] + cbuf[tx]
    xcopies = []
    for k in (1, 3, 2):
        tx, target = at_x(k)
        xcopies.append(pltpu.make_async_remote_copy(
            src_ref=merged.at[tx], dst_ref=xbuf.at[k - 1],
            send_sem=xs_sem.at[k - 1], recv_sem=xr_sem.at[k - 1],
            device_id=target, device_id_type=MESH))
    for copy in xcopies:
        copy.start()
    for copy in xcopies:
        copy.wait()
    total[...] = merged[x] + xbuf[0] + xbuf[1] + xbuf[2]
    zcopy = pltpu.make_async_remote_copy(
        src_ref=total.at[pl.ds(pl.multiple_of(40 * (1 - irrep), 8), 48), :], dst_ref=zbuf,
        send_sem=zs_sem, recv_sem=zr_sem, device_id=at_irrep, device_id_type=MESH)
    zcopy.start()
    zcopy.wait()
    out_ref[...] = total[pl.ds(pl.multiple_of(40 * irrep, 8), 48), :] + zbuf[...]


DMA = pltpu.SemaphoreType.DMA


def spread_call(owner, slab, part, hole):
    half = jnp.bfloat16
    return pl.pallas_call(
        spread_kernel,
        out_shape=(
            jax.ShapeDtypeStruct((NW, BLK, CHL), half),
            jax.ShapeDtypeStruct((YS, BLK, PACK), half),
            jax.ShapeDtypeStruct((ZS, YS, 80, 128), half),
        ),
        in_specs=[SM, VM, VM, VM],
        out_specs=(VM, VM, VM),
        scratch_shapes=[
            pltpu.VMEM((YS, BLK, CHL), half),
            pltpu.VMEM((NW, BLK, CHL), half),
            pltpu.VMEM((NW, BLK, CHL), half),
            pltpu.VMEM((NW, BLK, CHL), half),
            pltpu.VMEM((NW, BLK, CHL), half),
            DMA((3, NCH)), DMA((3, NCH)), DMA((3,)), DMA((3,)), DMA((3,)), DMA((3,)),
            DMA((NCH,)), DMA((NCH,)), DMA((NCH,)), DMA((NCH,)), DMA((7,)), DMA((7,)), DMA((3,)),
        ],
        compiler_params=pltpu.CompilerParams(
            collective_id=0, has_side_effects=True, vmem_limit_bytes=40 * 2**20),
    )(owner, slab, part, hole)


def work_call(place, first, second, hall, vsel, pall, coup, ea, ebc):
    half = jnp.bfloat16
    return pl.pallas_call(
        work_kernel,
        out_shape=jax.ShapeDtypeStruct((YS, BLK, PACK), jnp.float32),
        in_specs=[SM, SM, SM] + [VM] * 6,
        out_specs=VM,
        scratch_shapes=[
            pltpu.VMEM((2560, 128), jnp.float32),
            pltpu.VMEM((CHL, 160), half),
            pltpu.VMEM((BLK, CHL), jnp.float32),
            pltpu.VMEM((BLK, 128 * BCH), half),
            pltpu.VMEM((YS, PER * BLK, 128), half),
            pltpu.VMEM((NW, 160, 128 * YS * PER), half),
            pltpu.VMEM((BCH * BLK, 128 * YS * PER), jnp.float32),
            pltpu.VMEM((YS, PER * BLK, 128 * BCH), half),
            pltpu.VMEM((PER * BLK, 128), jnp.float32),
        ],
        compiler_params=pltpu.CompilerParams(vmem_limit_bytes=56 * 2**20),
    )(place, first, second, hall, vsel, pall, coup, ea, ebc)


def sum_call(code, contrib):
    single = jnp.float32
    return pl.pallas_call(
        sum_kernel,
        out_shape=jax.ShapeDtypeStruct((48, OUTL), single),
        in_specs=[VM, VM],
        out_specs=VM,
        scratch_shapes=[
            pltpu.VMEM((3, BLK, PACK), single),
            pltpu.VMEM((2, XS, BLK, OUTL), single),
            pltpu.VMEM((XS, BLK, OUTL), single),
            pltpu.VMEM((XS, BLK, OUTL), single),
            pltpu.VMEM((3, BLK, OUTL), single),
            pltpu.VMEM((BLK, OUTL), single),
            pltpu.VMEM((48, OUTL), single),
            DMA((3,)), DMA((3,)), DMA, DMA, DMA((3,)), DMA((3,)), DMA, DMA,
        ],
        compiler_params=pltpu.CompilerParams(
            collective_id=1, has_side_effects=True, vmem_limit_bytes=40 * 2**20),
    )(code, contrib)


def on_device(
    amplitudes, slabs, couplings, occ_energy, vir_energy, occ_irrep, pair_i, pair_j, window_k, owner
):
    half = jnp.bfloat16
    pair, beta, gamma, y, z = where_am_i()
    k_irrep = occ_irrep[window_k]
    pair_sym = occ_irrep[pair_i] ^ occ_irrep[pair_j]
    local = jnp.arange(PER)
    alpha = pair_sym[None, :] ^ k_irrep[:, None] ^ beta ^ gamma
    index = jnp.concatenate([(beta ^ pair_sym)[:, None], alpha.T], axis=1)
    blocks = jnp.take_along_axis(amplitudes, index[:, :, None], axis=1).reshape(PER, 1 + NW, BLK, BLK)
    send = blocks[:, 0].swapaxes(1, 2).reshape(PER, YS, BCH * BLK)
    tags = jnp.stack([pair_i, pair_j], axis=1).astype(half)[:, None, :]
    tail = jnp.pad(jnp.broadcast_to(tags, (PER, YS, 2)), ((0, 0), (0, 0), (0, CHL - BCH * BLK - 2)))
    hole = jnp.concatenate([send, tail], axis=2).swapaxes(0, 1).reshape(YS, PER * 16, 128)
    part = blocks[:, 1:].transpose(2, 1, 0, 3).reshape(BLK, NW * PER * BLK)
    part = jnp.pad(part, ((0, 0), (0, PACK - NW * PER * BLK)))
    slab = jnp.pad(slabs.reshape(BLK, BLK * BLK), ((0, 0), (0, LAST - BLK * BLK)))
    vsel, pall, hall = spread_call(owner, slab, part, hole)

    table = lax.dynamic_index_in_dim(hall, z, 0, keepdims=False).reshape(YS * PER, 16, 128)[:, 15, 16:18]
    first, second = table[:, 0].astype(jnp.int32), table[:, 1].astype(jnp.int32)
    sym = occ_irrep[first] ^ occ_irrep[second]
    alphas = sym[None, :] ^ k_irrep[:, None] ^ beta ^ gamma
    base = (occ_energy[first] + occ_energy[second])[None, :] + occ_energy[window_k][:, None]
    ea = (vir_energy[alphas] - base[:, :, None]).reshape(NW * YS, PER * BLK, 1)
    eb = lax.dynamic_slice_in_dim(jnp.take(vir_energy, beta, axis=0), y * BCH, BCH, 0)
    ec = jnp.take(vir_energy, gamma, axis=0)
    ebc = jnp.pad(eb[:, None] + ec[None, :], ((0, 0), (0, 128 - BLK)), constant_values=20.0)[:, None, :]
    keep = occ_irrep[None, :, None] ^ gamma ^ occ_irrep[None, None, :] ^ k_irrep[:, None, None]
    coup = jnp.where((keep == 0)[..., None], couplings, jnp.zeros_like(couplings))
    coup = jnp.pad(coup, ((0, 0), (0, 2), (0, 0), (0, 128 - BLK))).transpose(2, 1, 0, 3).reshape(30, 32, 256)
    contrib = work_call(
        jnp.reshape(y, (1,)), first, second, hall.reshape(2560, 128), vsel, pall, coup, ea, ebc)
    code = jnp.repeat(alpha, BLK, axis=1)
    code = jnp.pad(code, ((0, 0), (0, OUTL - PER * BLK)), constant_values=-1)
    result = sum_call(code, contrib)
    result = lax.dynamic_slice_in_dim(result, 4 * gamma, BLK // 2, 0)[:, :PER * BLK]
    return result.reshape(BLK // 2, PER, BLK).swapaxes(0, 1).reshape(PER, 1, BLK * BLK // 2)


def solution(mesh):
    placed = (
        P("pair", None, None),
        P("pair", "vtile", "irrep", None, None),
        P(None, None, None, "irrep"),
        P(),
        P(),
        P(),
        P("pair"),
        P("pair"),
        P(),
        P(),
    )
    return jax.shard_map(
        on_device,
        mesh=mesh,
        in_specs=placed,
        out_specs=P("pair", "vtile", "irrep"),
        check_vma=False,
    )
```

time: 1490 us -> 190 us (0.13)
  waiting for transfers between devices: 1000 us -> 0 us
  local copies, waits for them, and re-layouts: 214 us -> 20 us
  Pallas kernels: 0 us -> 165 us
  loops' own time: 88.4 us -> 0 us
  matrix products: 76.7 us -> 0 us
  other arithmetic: 53.1 us -> 4.54 us
  blocking collectives: 23.3 us -> 0 us
  between operations: 18.9 us -> 0.28 us
    psum x2 -> x0, waiting for transfers between devices: 820 us -> none  [the longest x1 459 us: spread(): return lax.psum(jnp.where(mine, shard, jnp.zeros_like(shard)), axis)]
    all_gather x1 -> x0, waiting for transfers between devices: 181 us -> none  [on_device(): lax.all_gather(outgoing, 'pair', axis=0, tiled=True)]
    pallas_call x0 -> x3, Pallas kernels: none -> 165 us  [the longest x1 72 us: spread_call(): pl.pallas_call(spread_kernel, out_shape=(jax.ShapeDtypeStruct((NW, BLK, C...]
    another operation x2 -> x0, loops' own time: 88.4 us -> none  [on_device(): contrib_all = lax.map(gathered_step, (amplitudes, pair_i, pair_j))]
    add x50 -> x0, local copies, waits for them, and re-layouts: 77.4 us -> none  [pair_term(): energy_a[:, :, None, None] + beta_energy[:, None, :, None]]
    dot_general x20 -> x0, matrix products: 76.7 us -> none  [the longest x10 50 us: pair_term(): jnp.einsum('max,mdx->mad', triples, slab_data, preferred_element_type=jnp...]
    reshape x10 -> x8, local copies, waits for them, and re-layouts: 50 us -> 2.8 us  [the longest x2 1.39 us: on_device(): jnp.pad(coup, ((0, 0), (0, 2), (0, 0), (0, 128 - BLK)))]
    sort x10 -> x0, other arithmetic: 31.7 us -> none  [gathered_step(): jnp.argsort(jnp.where(all_first == occ_i, 0, 1).astype(jnp.int32), stable...]
  transfers between devices with their start and end apart: 3 -> 0, of which waited for: 3 -> 0; matrix products, arithmetic and copies ran while one was open for 1% -> 0% of each run, Pallas kernels for 0% -> 0%
where the time goes in v1:
time: 190 us
  Pallas kernels  165 us (87%)
  local copies, waits for them, and re-layouts  20 us (11%)
  other arithmetic  4.54 us (2%)
    pallas_call x1, Pallas kernels, spread_call(): pl.pallas_call(spread_kernel, out_shape=(jax.ShapeDtypeStruct((NW, BLK, C...  72 us
    pallas_call x1, Pallas kernels, sum_call(): pl.pallas_call(sum_kernel, out_shape=jax.ShapeDtypeStruct((48, OUTL), sin...  48.9 us
    pallas_call x1, Pallas kernels, work_call(): pl.pallas_call(work_kernel, out_shape=jax.ShapeDtypeStruct((YS, BLK, PACK...  44.1 us
    unnamed x22, local copies, waits for them, and re-layouts  3.99 us

profile of v1, /device:TPU:1, one launch (start us, length us, event | category | flops | bytes accessed | tf_op | source)
XLA Modules:
  0.0 189.9 jit_solution(13475157720158739553)
XLA Ops:
  0.0 0.8 convert_bitcast_fusion.2
  0.8 1.3 gather_fusion
  2.1 1.3 gather_fusion.1
  3.4 0.7 compare_select_fusion.5
  4.1 0.6 gather_fusion.2
  5.0 1.4 gather_fusion.9
  6.4 0.5 gather.40
  6.9 0.2 copy.28
  7.4 0.1 reshape.401
  8.1 0.4 copy-done.9
  8.6 0.6 copy-done.5
  9.2 72.0 %shard_map.100 = (bf16[2,88,2048]{2,1,0:T(8,128)(2,1)S(1)}, bf16[4,88,896]{2,1,0:T(8,128)(2,1)S(1)}, bf16[8,4,80,128]{3,2,1,0:T(8,128)(2,1)S(1)}) custom-call(s32[2]{0:T(128)S(1)} %copy-done.5, bf16[88,7808]{1,0:T(8,128)(2,1)S(1)} %pad.25.slab_ref, bf16[88,896]{1,0:T(8,128)(2,1)S(1)} %pad.26.part_ref, bf16[4,80,128]{2,1,0:T(8,128)(2,1)S(1)} %reshape.402.hole_ref), custom_call_target="tpu_custom_call" | custom-call | tf_op jit(solution)/shard_map/pallas_call | solution.py:390
  81.2 0.8 copy-done.3
  82.1 0.8 copy-done.4
  83.2 0.7 gather_fusion.6
  83.9 0.7 gather_fusion.7
  84.6 0.6 gather_fusion.8
  85.3 0.7 gather_fusion.3
  86.0 0.7 gather_fusion.4
  86.9 0.6 gather_fusion.5
  87.6 1.8 sub.26.ea_ref
  89.4 0.6 convert_bitcast_fusion
  90.1 0.6 broadcast_in_dim.79.ebc_ref
  90.8 0.2 xor_compare_fusion
  91.0 1.4 broadcast_select_fusion
  92.4 0.5 pad_bitcast_fusion
  92.9 0.3 reshape.539
  93.3 1.1 copy.37.coup_ref
  94.3 44.1 %shard_map.101.c_ref = f32[4,88,896]{2,1,0:T(8,128)} custom-call(s32[1]{0:T(128)} %bitcast.place_ref, s32[20]{0:T(128)} %get-tuple-element.30.first_ref, s32[20]{0:T(128)} %get-tuple-element.29.second_ref, bf16[2560,128]{1,0:T(8,128)(2,1)} %bitcast.47, bf16[2,88,2048]{2,1,0:T(8,128)(2,1)} %copy-done.3, bf16[4,88,896]{2,1,0:T(8,128)(2,1)} %copy-done.4, ...), custom_call_target="tpu_custom_call" | custom-call | tf_op jit(solution)/shard_map/pallas_call | solution.py:415
  138.7 1.3 copy-done.1
  140.0 48.9 %shard_map.102 = f32[48,512]{1,0:T(8,128)S(1)} custom-call(s32[2,512]{1,0:T(2,128)S(1)} %pad.24.code_ref, f32[4,88,896]{2,1,0:T(8,128)S(1)} %copy-done.1), custom_call_target="tpu_custom_call" | custom-call | tf_op jit(solution)/shard_map/pallas_call | solution.py:437
  189.1 0.8 reshape.540
  (67 shorter events, 2.4 us)
Async XLA Ops:
  0.0 5.0 %copy-start = (bf16[5,8,7744]{2,1,0:T(8,128)(2,1)S(1)}, bf16[5,8,7744]{2,1,0:T(8,128)(2,1)}, u32[]{:S(2)}) copy-start(bf16[5,8,7744]{2,1,0:T(8,128)(2,1)} %param.12) | copy-start | bytes 1858564
  0.0 4.1 %copy-start.6 = (s32[30]{0:T(128)S(1)}, s32[30]{0:T(128)}, u32[]{:S(2)}) copy-start(s32[30]{0:T(128)} %param.17) | copy-start | bytes 364
  7.2 1.3 copy-start.9
  8.5 0.7 copy-start.5
  9.2 74.0 %copy-start.7 = (f32[30]{0:T(128)S(1)}, f32[30]{0:T(128)}, u32[]{:S(2)}) copy-start(f32[30]{0:T(128)} %param.15) | copy-start | bytes 364
  81.2 0.9 copy-start.3
  82.1 0.8 copy-start.4
  82.9 3.8 %copy-start.2 = (bf16[8,4,80,128]{3,2,1,0:T(8,128)(2,1)}, bf16[8,4,80,128]{3,2,1,0:T(8,128)(2,1)S(1)}, u32[]{:S(2)}) copy-start(bf16[8,4,80,128]{3,2,1,0:T(8,128)(2,1)S(1)} %get-tuple-element.9) | copy-start | bytes 1966084
  82.9 4.0 %copy-start.8 = (f32[8,88]{1,0:T(8,128)S(1)}, f32[8,88]{1,0:T(8,128)}, u32[]{:S(2)}) copy-start(f32[8,88]{1,0:T(8,128)} %param.16) | copy-start | bytes 8452
  86.0 5.0 %copy-start.10 = (bf16[2,30,30,88]{3,0,2,1:T(2,128)(2,1)S(1)}, bf16[2,30,30,88]{3,0,2,1:T(2,128)(2,1)}, u32[]{:S(2)}) copy-start(bf16[2,30,30,88]{3,0,2,1:T(2,128)(2,1)} %param.14) | copy-start | bytes 950404
  138.7 1.3 copy-start.1

commit v2 on v1

v2 whole, which is shorter than its diff:
```python
import jax
import jax.numpy as jnp
from jax import lax
from jax.experimental import pallas as pl
from jax.experimental.pallas import tpu as pltpu
from jax.sharding import PartitionSpec as P

MESH = pl.DeviceIdType.MESH
YS, ZS, XS = 4, 8, 4
BLK = 88
PER = 5
NW = 2
BCH = BLK // YS
CHL = 2048
TILES = 16
ALL = 61
YPER = 2
YN = TILES // YPER
SKEW = 4
RING = 8
RIGHT, LEFT = 4, 3
PACK = 896
OUTL = 512
VM = pl.BlockSpec(memory_space=pltpu.VMEM)
SM = pl.BlockSpec(memory_space=pltpu.SMEM)


def where_am_i():
    pair, vtile, irrep = lax.axis_index("pair"), lax.axis_index("vtile"), lax.axis_index("irrep")
    return pair, vtile, irrep, lax.rem(pair, YS), pair // YS


def spread_kernel(
    owner_ref, slab_ref, part_ref, hole_ref,
    vsel_ref, pall_ref, hall_ref,
    tiles, ybuf, frecv, brecv, fsend, bsend,
    ys_sem, yr_sem, hs_sem, hr_sem, ps_sem, pr_sem,
    fs_sem, fr_sem, bs_sem, br_sem, zs_sem, zr_sem, local_sem,
):
    pair, vtile, irrep, y, z = where_am_i()
    zg = irrep * ZS + z

    def at_y(k):
        ty = lax.rem(y + k + YS, YS)
        return ty, (z * YS + ty, vtile, irrep)

    def at_z(step):
        tz = lax.rem(zg + step + 2 * ZS, 2 * ZS)
        return (lax.rem(tz, ZS) * YS + y, vtile, tz // ZS)

    barrier = pltpu.get_barrier_semaphore()
    for k in (1, 2, 3):
        pl.semaphore_signal(barrier, inc=1, device_id=at_y(k)[1], device_id_type=MESH)
    for step in (1, -1):
        pl.semaphore_signal(barrier, inc=1, device_id=at_z(step), device_id_type=MESH)
    for t in range(ALL - 1):
        tiles[t] = slab_ref[:, 128 * t:128 * t + 128]
    tiles[ALL - 1] = jnp.zeros((BLK, 128), jnp.bfloat16)
    tiles[ALL - 1, :, :64] = slab_ref[:, 128 * (ALL - 1):]
    pl.semaphore_wait(barrier, 5)

    def hole_copy(k):
        ty, target = at_y(k)
        return pltpu.make_async_remote_copy(
            src_ref=hole_ref.at[ty], dst_ref=hall_ref.at[z, y],
            send_sem=hs_sem.at[k - 1], recv_sem=hr_sem.at[k - 1],
            device_id=target, device_id_type=MESH)

    def part_copy(k):
        _, target = at_y(k)
        return pltpu.make_async_remote_copy(
            src_ref=part_ref, dst_ref=pall_ref.at[y],
            send_sem=ps_sem.at[k - 1], recv_sem=pr_sem.at[k - 1],
            device_id=target, device_id_type=MESH)

    def slab_copy(k, n):
        ty, target = at_y(k)
        return pltpu.make_async_remote_copy(
            src_ref=tiles.at[pl.ds(ty * 15 + n * YPER, YPER)],
            dst_ref=ybuf.at[y, pl.ds(n * YPER, YPER)],
            send_sem=ys_sem.at[k - 1, n], recv_sem=yr_sem.at[k - 1, n],
            device_id=target, device_id_type=MESH)

    def ring_copy(index):
        step = index if index < RIGHT else index - RIGHT
        right = index < RIGHT
        held = lax.rem(zg + (-step if right else step) + 2 * ZS, ZS)
        return pltpu.make_async_remote_copy(
            src_ref=hall_ref.at[held], dst_ref=hall_ref.at[held],
            send_sem=zs_sem.at[index], recv_sem=zr_sem.at[index],
            device_id=at_z(1 if right else -1), device_id_type=MESH)

    def chain_copy(forward, n):
        src, dst = (fsend, frecv) if forward else (bsend, brecv)
        send, recv = (fs_sem, fr_sem) if forward else (bs_sem, br_sem)
        tz = jnp.minimum(z + 1, ZS - 1) if forward else jnp.maximum(z - 1, 0)
        return pltpu.make_async_remote_copy(
            src_ref=src.at[n], dst_ref=dst.at[n],
            send_sem=send.at[n], recv_sem=recv.at[n],
            device_id=(tz * YS + y, vtile, irrep), device_id_type=MESH)

    for k in (1, 3, 2):
        hole_copy(k).start()

    def send_chunk(n, _):
        for k in (1, 3, 2):
            slab_copy(k, n).start()
        return 0

    lax.fori_loop(0, YN, send_chunk, 0)
    for k in (1, 3, 2):
        part_copy(k).start()

    own_slab = pltpu.make_async_copy(tiles.at[pl.ds(y * 15, TILES)], ybuf.at[y], local_sem.at[0])
    own_part = pltpu.make_async_copy(part_ref, pall_ref.at[y], local_sem.at[1])
    own_hole = pltpu.make_async_copy(hole_ref.at[y], hall_ref.at[z, y], local_sem.at[2])
    for copy in (own_hole, own_slab, own_part):
        copy.start()
    own_hole.wait()
    for k in (1, 2, 3):
        hole_copy(k).wait_recv()
    ring_copy(0).start()
    ring_copy(RIGHT).start()
    own_slab.wait()
    own_part.wait()

    root_y = [lax.rem(owner_ref[w], YS) for w in range(NW)]
    root_z = [owner_ref[w] // YS for w in range(NW)]

    def candidate(w, n):
        value = ybuf[0, n]
        for source in range(1, YS):
            value = jnp.where(root_y[w] == source, ybuf[source, n], value)
        return value

    def chain_event(forward, n):
        src, dst = (fsend, frecv) if forward else (bsend, brecv)
        first_here = z <= 3 if forward else z >= 4
        start, end = (z == 0, z == ZS - 1) if forward else (z == ZS - 1, z == 0)

        @pl.when(jnp.logical_and(first_here, lax.rem(n, YPER) == 0))
        def _():
            for k in (1, 2, 3):
                slab_copy(k, n // YPER).wait_recv()

        mine = [candidate(w, n) for w in range(NW)]

        @pl.when(start)
        def _():
            for w in range(NW):
                dst[n, w] = mine[w]

        @pl.when(jnp.logical_not(start))
        def _():
            chain_copy(forward, n).wait_recv()

        if forward:
            for w in range(NW):
                vsel_ref[n, w] = mine[w]

        @pl.when(jnp.logical_not(end))
        def _():
            for w in range(NW):
                src[n, w] = jnp.where(root_z[w] == z, mine[w], dst[n, w])
            chain_copy(forward, n).start()

    def chain_step(t, _):
        nf = t - SKEW * z
        nb = t - SKEW * (ZS - 1 - z)

        @pl.when(jnp.logical_and(nf >= 0, nf < TILES))
        def _():
            chain_event(True, nf)

        @pl.when(jnp.logical_and(nb >= 0, nb < TILES))
        def _():
            chain_event(False, nb)

        for step in range(1, RIGHT):
            @pl.when(t == RING * step)
            def _():
                ring_copy(step - 1).wait_recv()
                ring_copy(step).start()
                if step < LEFT:
                    ring_copy(RIGHT + step - 1).wait_recv()
                    ring_copy(RIGHT + step).start()
        return 0

    lax.fori_loop(0, TILES + SKEW * (ZS - 1), chain_step, 0)

    def settle(n, _):
        for w in range(NW):
            other = jnp.where(root_z[w] < z, frecv[n, w], brecv[n, w])
            vsel_ref[n, w] = jnp.where(root_z[w] == z, vsel_ref[n, w], other)
        return 0

    lax.fori_loop(0, TILES, settle, 0)

    for k in (1, 2, 3):
        part_copy(k).wait_recv()
    ring_copy(RIGHT - 1).wait_recv()
    ring_copy(RIGHT + LEFT - 1).wait_recv()

    def sent(n, _):
        @pl.when(z < ZS - 1)
        def _():
            chain_copy(True, n).wait_send()

        @pl.when(z > 0)
        def _():
            chain_copy(False, n).wait_send()

        return 0

    lax.fori_loop(0, TILES, sent, 0)

    def sent_y(n, _):
        for k in (1, 2, 3):
            slab_copy(k, n).wait_send()
        return 0

    lax.fori_loop(0, YN, sent_y, 0)
    for k in (1, 2, 3):
        hole_copy(k).wait_send()
        part_copy(k).wait_send()
    for index in range(RIGHT + LEFT):
        ring_copy(index).wait_send()


def window_of(offset, width):
    base = offset // 128 * 128
    return base, 128 if offset - base + width <= 128 else 256


def cut(value, offset):
    moved = pltpu.roll(value, value.shape[1] - offset, 1) if offset else value
    moved = moved[:, :128]
    lane = lax.broadcasted_iota(jnp.int32, moved.shape, 1)
    return jnp.where(lane < BLK, moved, 0.0)


def work_kernel(
    first_ref, second_ref, irrep_ref, occ_ref, window_ref, vir_ref,
    hall_ref, vsel_ref, pall_ref, coup_ref, column_ref, row_ref,
    out_ref,
    wide, left, vshift, vt, vback, amp, weight, holes, column, acc,
    part0, part1, trip0, trip1, contrib,
    ybuf, slots, cbuf, merged, xbuf, total, zbuf,
    ys_sem, yr_sem, cs_sem, cr_sem, xs_sem, xr_sem, zs_sem, zr_sem,
):
    half, single = jnp.bfloat16, jnp.float32
    pair, vtile, irrep, y, z = where_am_i()
    x, core = vtile // 2, lax.rem(vtile, 2)

    def at_y(k):
        ty = lax.rem(y + k, YS)
        return ty, (z * YS + ty, vtile, irrep)

    def at_x(k):
        tx = lax.rem(x + k, XS)
        return tx, (pair, tx * 2 + core, irrep)

    at_core = (pair, x * 2 + 1 - core, irrep)
    at_irrep = (pair, vtile, 1 - irrep)
    barrier = pltpu.get_barrier_semaphore()
    for k in (1, 2, 3):
        pl.semaphore_signal(barrier, inc=1, device_id=at_y(k)[1], device_id_type=MESH)
        pl.semaphore_signal(barrier, inc=1, device_id=at_x(k)[1], device_id_type=MESH)
    pl.semaphore_signal(barrier, inc=1, device_id=at_core, device_id_type=MESH)
    pl.semaphore_signal(barrier, inc=1, device_id=at_irrep, device_id_type=MESH)

    wide[...] = hall_ref[...].astype(single)
    for k in range(16):
        tile = wide[pl.ds(k, 160, stride=16), :]
        left[128 * k:128 * k + 128, :] = tile.T.astype(half)
    table = wide[pl.ds(15, 160, stride=16), :]
    group, member = table[:, 16:17], table[:, 17:18]
    slot = lax.broadcasted_iota(jnp.int32, (160, 32), 1).astype(single)
    for p in range(YS * PER):
        here = jnp.logical_and(member == slot, group == first_ref[p].astype(single))
        pick = here.astype(single).astype(half)
        weight[:, 256 * p:256 * p + 256] = jnp.dot(
            pick, coup_ref[second_ref[p]], preferred_element_type=single).astype(half)

    for w in range(NW):
        for shift in range(YS):
            @pl.when(y == shift)
            def _():
                for t in range(TILES):
                    vshift[:, 128 * t:128 * t + 128] = vsel_ref[t, w].astype(single)
                if shift:
                    vshift[...] = pltpu.roll(vshift[...], CHL - 16 * shift, 1)
        for b in range(BCH):
            base, width = window_of(BLK * b, BLK)
            tile = cut(vshift[:, base:base + width], BLK * b - base)
            vt[w, :, 128 * b:128 * b + 128] = tile.astype(half)
            vback[w, 128 * b:128 * b + 128, :BLK] = tile.T.astype(half)
        for source in range(YS):
            parts = []
            for p in range(PER):
                offset = BLK * (w * PER + p)
                base, width = window_of(offset, BLK)
                parts.append(cut(pall_ref[source, :, base:base + width].astype(single), offset - base))
            amp[w, source] = jnp.concatenate(parts, axis=0).astype(half)
    vback[:, :, BLK:] = jnp.zeros((NW, 128 * BCH, 128 - BLK), half)
    contrib[:, :, 880:PACK] = jnp.zeros((YS, BLK, PACK - 880), single)
    pl.semaphore_wait(barrier, 8)

    def alpha_of(q, w):
        sym = irrep_ref[first_ref[q]] ^ irrep_ref[second_ref[q]]
        return sym ^ irrep_ref[window_ref[w]] ^ vtile ^ irrep

    def ycopy(k):
        ty, target = at_y(k)
        return pltpu.make_async_remote_copy(
            src_ref=contrib.at[ty], dst_ref=ybuf.at[k - 1],
            send_sem=ys_sem.at[k - 1], recv_sem=yr_sem.at[k - 1],
            device_id=target, device_id_type=MESH)

    gamma_row = row_ref[irrep]

    def source_step(index, _):
        source = lax.rem(y + index + 1, YS)

        def hole_step(p, _):
            lanes = pl.ds(pl.multiple_of(p * 256, 256), 256)
            mine = pl.ds(pl.multiple_of((source * PER + p) * 256, 256), 256)
            holes[:, lanes] = jnp.dot(left[:BCH * BLK, :], weight[:, mine], preferred_element_type=single)
            return 0

        lax.fori_loop(0, PER, hole_step, 0)
        for w in range(NW):
            for p in range(PER):
                q = source * PER + p
                base = occ_ref[first_ref[q]] + occ_ref[second_ref[q]] + occ_ref[window_ref[w]]
                column[BLK * p:BLK * p + BLK, :] = column_ref[alpha_of(q, w)] - base

            def lanes_of(t):
                return pl.ds(pl.multiple_of(t * 256, 256), 256)

            def particle(t):
                return jnp.dot(amp[w, source, :, :BLK], vt[w, :, lanes_of(t)], preferred_element_type=single)

            def stage(t, now, later, fill, drain):
                if later is not None:
                    later[...] = particle(t + 1)
                acc[...] += jnp.dot(
                    drain[...], vback[w, lanes_of(jnp.maximum(t - 1, 0)), :], preferred_element_type=single)
                for side in range(2):
                    b = 2 * t + side
                    rows = pl.ds(pl.multiple_of(b * BLK, 8), BLK)
                    hole = jnp.concatenate([
                        holes[rows, 256 * p + 128 * w:256 * p + 128 * w + 128] for p in range(PER)], axis=0)
                    energy = gamma_row + vir_ref[vtile, y * BCH + b]
                    inverse = pltpu.reciprocal(column[...] + energy, approx=True)
                    fill[:, 128 * side:128 * side + 128] = (
                        (now[:, 128 * side:128 * side + 128] - hole) * inverse).astype(half)

            acc[...] = jnp.zeros_like(acc)
            trip1[...] = jnp.zeros_like(trip1)
            part0[...] = particle(0)

            def two_steps(u, _):
                stage(2 * u, part0, part1, trip0, trip1)
                stage(2 * u + 1, part1, part0, trip1, trip0)
                return 0

            lax.fori_loop(0, BCH // 4, two_steps, 0)
            stage(BCH // 2 - 1, part0, None, trip0, trip1)
            acc[...] += jnp.dot(trip0[...], vback[w, 128 * (BCH - 2):, :], preferred_element_type=single)
            for p in range(PER):
                offset = BLK * (w * PER + p)
                contrib[source, :, offset:offset + BLK] = acc[BLK * p:BLK * p + BLK, :BLK]

        @pl.when(index < YS - 1)
        def _():
            ty, target = at_y(index + 1)
            pltpu.make_async_remote_copy(
                src_ref=contrib.at[ty], dst_ref=ybuf.at[index],
                send_sem=ys_sem.at[index], recv_sem=yr_sem.at[index],
                device_id=target, device_id_type=MESH).start()

        return 0

    lax.fori_loop(0, YS, source_step, 0)
    for k in (1, 2, 3):
        ycopy(k).wait()
    summed = contrib[y] + ybuf[0] + ybuf[1] + ybuf[2]
    windows = [summed[:, :OUTL], pltpu.roll(summed, PACK - 440, 1)[:, :OUTL]]
    lane = lax.broadcasted_iota(jnp.int32, (1, OUTL), 1)
    codes = []
    for w in range(NW):
        code = jnp.full((1, OUTL), -1, jnp.int32)
        for p in range(PER):
            inside = jnp.logical_and(lane >= BLK * p, lane < BLK * (p + 1))
            code = jnp.where(inside, alpha_of(y * PER + p, w), code)
        codes.append(code)
    for target in range(2 * XS):
        slots[target % 2, target // 2] = sum(
            jnp.where(codes[w] == target, windows[w], 0.0) for w in range(NW))
    ccopy = pltpu.make_async_remote_copy(
        src_ref=slots.at[1 - core], dst_ref=cbuf,
        send_sem=cs_sem, recv_sem=cr_sem, device_id=at_core, device_id_type=MESH)
    ccopy.start()
    ccopy.wait()
    for tx in range(XS):
        merged[tx] = slots[core, tx] + cbuf[tx]
    xcopies = []
    for k in (1, 3, 2):
        tx, target = at_x(k)
        xcopies.append(pltpu.make_async_remote_copy(
            src_ref=merged.at[tx], dst_ref=xbuf.at[k - 1],
            send_sem=xs_sem.at[k - 1], recv_sem=xr_sem.at[k - 1],
            device_id=target, device_id_type=MESH))
    for copy in xcopies:
        copy.start()
    for copy in xcopies:
        copy.wait()
    total[...] = merged[x] + xbuf[0] + xbuf[1] + xbuf[2]
    zcopy = pltpu.make_async_remote_copy(
        src_ref=total.at[pl.ds(pl.multiple_of(40 * (1 - irrep), 8), 48), :], dst_ref=zbuf,
        send_sem=zs_sem, recv_sem=zr_sem, device_id=at_irrep, device_id_type=MESH)
    zcopy.start()
    zcopy.wait()
    out_ref[...] = total[pl.ds(pl.multiple_of(40 * irrep, 8), 48), :] + zbuf[...]


DMA = pltpu.SemaphoreType.DMA


def spread_call(owner, slab, part, hole):
    half = jnp.bfloat16
    return pl.pallas_call(
        spread_kernel,
        out_shape=(
            jax.ShapeDtypeStruct((TILES, NW, BLK, 128), half),
            jax.ShapeDtypeStruct((YS, BLK, PACK), half),
            jax.ShapeDtypeStruct((ZS, YS, 80, 128), half),
        ),
        in_specs=[SM, VM, VM, VM],
        out_specs=(VM, VM, VM),
        scratch_shapes=[
            pltpu.VMEM((ALL, BLK, 128), half),
            pltpu.VMEM((YS, TILES, BLK, 128), half),
            pltpu.VMEM((TILES, NW, BLK, 128), half),
            pltpu.VMEM((TILES, NW, BLK, 128), half),
            pltpu.VMEM((TILES, NW, BLK, 128), half),
            pltpu.VMEM((TILES, NW, BLK, 128), half),
            DMA((3, YN)), DMA((3, YN)), DMA((3,)), DMA((3,)), DMA((3,)), DMA((3,)),
            DMA((TILES,)), DMA((TILES,)), DMA((TILES,)), DMA((TILES,)), DMA((7,)), DMA((7,)), DMA((3,)),
        ],
        compiler_params=pltpu.CompilerParams(
            collective_id=0, has_side_effects=True, vmem_limit_bytes=40 * 2**20),
    )(owner, slab, part, hole)


def work_call(first, second, irreps, occ, window, vir, hall, vsel, pall, coup, columns, rows):
    half, single = jnp.bfloat16, jnp.float32
    return pl.pallas_call(
        work_kernel,
        out_shape=jax.ShapeDtypeStruct((48, OUTL), single),
        in_specs=[SM] * 6 + [VM] * 6,
        out_specs=VM,
        scratch_shapes=[
            pltpu.VMEM((2560, 128), single),
            pltpu.VMEM((CHL, 160), half),
            pltpu.VMEM((BLK, CHL), single),
            pltpu.VMEM((NW, BLK, 128 * BCH), half),
            pltpu.VMEM((NW, 128 * BCH, 128), half),
            pltpu.VMEM((NW, YS, PER * BLK, 128), half),
            pltpu.VMEM((160, 256 * YS * PER), half),
            pltpu.VMEM((BCH * BLK, 256 * PER), single),
            pltpu.VMEM((PER * BLK, 128), single),
            pltpu.VMEM((PER * BLK, 128), single),
            pltpu.VMEM((PER * BLK, 256), single),
            pltpu.VMEM((PER * BLK, 256), single),
            pltpu.VMEM((PER * BLK, 256), half),
            pltpu.VMEM((PER * BLK, 256), half),
            pltpu.VMEM((YS, BLK, PACK), single),
            pltpu.VMEM((3, BLK, PACK), single),
            pltpu.VMEM((2, XS, BLK, OUTL), single),
            pltpu.VMEM((XS, BLK, OUTL), single),
            pltpu.VMEM((XS, BLK, OUTL), single),
            pltpu.VMEM((3, BLK, OUTL), single),
            pltpu.VMEM((BLK, OUTL), single),
            pltpu.VMEM((48, OUTL), single),
            DMA((3,)), DMA((3,)), DMA, DMA, DMA((3,)), DMA((3,)), DMA, DMA,
        ],
        compiler_params=pltpu.CompilerParams(
            collective_id=1, has_side_effects=True, vmem_limit_bytes=56 * 2**20),
    )(first, second, irreps, occ, window, vir, hall, vsel, pall, coup, columns, rows)


def pick(table, index):
    places = jnp.arange(table.shape[0], dtype=jnp.int32)
    return jnp.sum(jnp.where(index[..., None] == places, table, 0), axis=-1)


def on_device(
    amplitudes, slabs, couplings, occ_energy, vir_energy, occ_irrep, pair_i, pair_j, window_k, owner
):
    half = jnp.bfloat16
    pair, beta, gamma, y, z = where_am_i()
    k_irrep = pick(occ_irrep, window_k)
    pair_sym = pick(occ_irrep, pair_i) ^ pick(occ_irrep, pair_j)
    alpha = pair_sym[None, :] ^ k_irrep[:, None] ^ beta ^ gamma
    index = jnp.concatenate([(beta ^ pair_sym)[:, None], alpha.T], axis=1)
    blocks = jnp.take_along_axis(amplitudes, index[:, :, None], axis=1).reshape(PER, 1 + NW, BLK, BLK)
    send = blocks[:, 0].swapaxes(1, 2).reshape(PER, YS, BCH * BLK)
    tags = jnp.stack([pair_i, pair_j], axis=1).astype(half)[:, None, :]
    tail = jnp.pad(jnp.broadcast_to(tags, (PER, YS, 2)), ((0, 0), (0, 0), (0, CHL - BCH * BLK - 2)))
    hole = jnp.concatenate([send, tail], axis=2).swapaxes(0, 1).reshape(YS, PER * 16, 128)
    part = blocks[:, 1:].transpose(2, 1, 0, 3).reshape(BLK, NW * PER * BLK)
    part = jnp.pad(part, ((0, 0), (0, PACK - NW * PER * BLK)))
    vsel, pall, hall = spread_call(owner, slabs.reshape(BLK, BLK * BLK), part, hole)

    table = lax.dynamic_index_in_dim(hall, z, 0, keepdims=False).reshape(YS * PER, 16, 128)[:, 15, 16:18]
    first, second = table[:, 0].astype(jnp.int32), table[:, 1].astype(jnp.int32)
    columns = jnp.broadcast_to(vir_energy[:, :, None], (8, BLK, 128))
    rows = jnp.pad(vir_energy, ((0, 0), (0, 128 - BLK)), constant_values=20.0)[:, None, :]
    keep = occ_irrep[None, :, None] ^ gamma ^ occ_irrep[None, None, :] ^ k_irrep[:, None, None]
    coup = jnp.where((keep == 0)[..., None], couplings, jnp.zeros_like(couplings))
    coup = jnp.pad(coup, ((0, 0), (0, 2), (0, 0), (0, 128 - BLK))).transpose(2, 1, 0, 3).reshape(30, 32, 256)
    result = work_call(
        first, second, occ_irrep, occ_energy, window_k, vir_energy,
        hall.reshape(2560, 128), vsel, pall, coup, columns, rows)
    result = lax.dynamic_slice_in_dim(result, 4 * gamma, BLK // 2, 0)[:, :PER * BLK]
    return result.reshape(BLK // 2, PER, BLK).swapaxes(0, 1).reshape(PER, 1, BLK * BLK // 2)


def solution(mesh):
    placed = (
        P("pair", None, None),
        P("pair", "vtile", "irrep", None, None),
        P(None, None, None, "irrep"),
        P(),
        P(),
        P(),
        P("pair"),
        P("pair"),
        P(),
        P(),
    )
    return jax.shard_map(
        on_device,
        mesh=mesh,
        in_specs=placed,
        out_specs=P("pair", "vtile", "irrep"),
        check_vma=False,
    )
```

time: 190 us -> 141 us (0.74)
  Pallas kernels: 165 us -> 126 us
  local copies, waits for them, and re-layouts: 20 us -> 10.4 us
    pallas_call x3 -> x2, Pallas kernels: 165 us -> 126 us  [the longest x1 69 us: work_call(): pl.pallas_call(work_kernel, out_shape=jax.ShapeDtypeStruct((48, OUTL), si...]
    gather x10 -> x0, local copies, waits for them, and re-layouts: 7.26 us -> none  [the longest x2 2.6 us: on_device(): pair_sym = occ_irrep[pair_i] ^ occ_irrep[pair_j]]
where the time goes in v2:
time: 141 us
  Pallas kernels  126 us (89%)
  local copies, waits for them, and re-layouts  10.4 us (7%)
  other arithmetic  4.49 us (3%)
    pallas_call x1, Pallas kernels, work_call(): pl.pallas_call(work_kernel, out_shape=jax.ShapeDtypeStruct((48, OUTL), si...  69 us
    pallas_call x1, Pallas kernels, spread_call(): pl.pallas_call(spread_kernel, out_shape=(jax.ShapeDtypeStruct((TILES, NW,...  57 us

profile of v2, /device:TPU:1, one launch (start us, length us, event | category | flops | bytes accessed | tf_op | source)
XLA Modules:
  0.0 141.1 jit_solution(13185898959103637372)
XLA Ops:
  0.0 1.0 select_reduce_fusion
  1.0 0.9 fusion.6
  1.8 0.1 fusion.7
  1.9 0.1 copy.36
  2.0 0.1 reshape.287
  2.1 1.4 gather_fusion
  3.5 0.5 gather.7
  4.0 0.2 copy.37
  4.3 0.1 broadcast_select_fusion.1
  4.5 0.1 reshape.278
  4.7 0.1 copy.39
  4.8 0.1 fusion.2
  5.0 0.1 reshape.279.hole_ref
  5.1 0.1 copy.38
  5.3 0.4 copy-done.1
  5.7 57.0 %shard_map.100 = (bf16[16,2,88,128]{3,2,1,0:T(8,128)(2,1)S(1)}, bf16[4,88,896]{2,1,0:T(8,128)(2,1)S(1)}, bf16[8,4,80,128]{3,2,1,0:T(8,128)(2,1)S(1)}) custom-call(s32[2]{0:T(128)S(1)} %copy-done.5, bf16[88,7744]{1,0:T(8,128)(2,1)S(1)} %bitcast.39, bf16[88,896]{1,0:T(8,128)(2,1)S(1)} %pad.16.part_ref, bf16[4,80,128]{2,1,0:T(8,128)(2,1)S(1)} %reshape.279.hole_ref), custom_call_target="tpu_custom_call" | custom-call | tf_op jit(solution)/shard_map/pallas_call | solution.py:433
  62.6 0.9 copy-done.3
  63.5 0.8 copy-done.4
  64.3 0.1 slice.28
  64.4 0.1 copy.41
  64.5 0.6 bitcast_convert_fusion
  65.2 0.2 xor_compare_fusion
  65.4 1.4 broadcast_select_fusion
  66.8 0.5 pad_bitcast_fusion
  67.3 0.3 reshape.294
  67.6 1.1 copy.45.coup_ref
  68.7 0.9 broadcast_in_dim.75.column_ref
  69.6 0.6 pad.19
  70.2 69.0 %shard_map.101 = f32[48,512]{1,0:T(8,128)} custom-call(s32[20]{0:T(128)} %get-tuple-element.16.first_ref, s32[20]{0:T(128)} %get-tuple-element.15.second_ref, s32[30]{0:T(128)} %irrep_ref.1, f32[30]{0:T(128)} %occ_ref.1, s32[2]{0:T(128)} %window_ref.1, f32[8,88]{1,0:T(8,128)} %vir_ref.1, bf16[2560,128]{1,0:T(8,128)(2,1)} %bitcast.40, ...), custom_call_target="tpu_custom_call" | custom-call | tf_op jit(solution)/shard_map/pallas_call | solution.py:459
  139.2 0.9 constant_dynamic-slice_fusion.1
  140.1 0.1 reshape.283
  140.3 0.8 reshape.295
  (35 shorter events, 0.4 us)
Async XLA Ops:
  0.0 2.1 %copy-start = (bf16[5,8,7744]{2,1,0:T(8,128)(2,1)S(1)}, bf16[5,8,7744]{2,1,0:T(8,128)(2,1)}, u32[]{:S(2)}) copy-start(bf16[5,8,7744]{2,1,0:T(8,128)(2,1)} %param.10) | copy-start | bytes 1858564
  3.5 1.2 copy-start.9
  3.5 1.2 copy-start.10
  4.3 1.3 copy-start.1
  4.3 1.3 copy-start.5
  5.1 60.0 %copy-start.8 = (s32[30]{0:T(128)S(1)}, s32[30]{0:T(128)}, u32[]{:S(2)}) copy-start(s32[30]{0:T(128)} %irrep_ref.1) | copy-start | bytes 364
  5.1 60.3 %copy-start.6 = (bf16[2,30,30,88]{3,0,2,1:T(2,128)(2,1)S(1)}, bf16[2,30,30,88]{3,0,2,1:T(2,128)(2,1)}, u32[]{:S(2)}) copy-start(bf16[2,30,30,88]{3,0,2,1:T(2,128)(2,1)} %param.12) | copy-start | bytes 950404
  62.6 0.9 copy-start.3
  63.5 0.8 copy-start.4
  64.3 3.3 %copy-start.2 = (bf16[8,4,80,128]{3,2,1,0:T(8,128)(2,1)}, bf16[8,4,80,128]{3,2,1,0:T(8,128)(2,1)S(1)}, u32[]{:S(2)}) copy-start(bf16[8,4,80,128]{3,2,1,0:T(8,128)(2,1)S(1)} %get-tuple-element.8) | copy-start | bytes 1966084
  66.8 1.9 %copy-start.7 = (f32[8,88]{1,0:T(8,128)S(1)}, f32[8,88]{1,0:T(8,128)}, u32[]{:S(2)}) copy-start(f32[8,88]{1,0:T(8,128)} %vir_ref.1) | copy-start | bytes 8452

commit v3 on v2

--- a/solution.py
+++ b/solution.py
@@ -17,7 +17,9 @@
 YPER = 2
 YN = TILES // YPER
 SKEW = 4
-RING = 8
+RING = 4
+WEIGHTS = RING * 4 + 5
+HOLES = WEIGHTS + 4
 RIGHT, LEFT = 4, 3
 PACK = 896
 OUTL = 512
@@ -30,14 +32,34 @@
     return pair, vtile, irrep, lax.rem(pair, YS), pair // YS
 
 
-def spread_kernel(
-    owner_ref, slab_ref, part_ref, hole_ref,
-    vsel_ref, pall_ref, hall_ref,
-    tiles, ybuf, frecv, brecv, fsend, bsend,
+def window_of(offset, width):
+    base = offset // 128 * 128
+    return base, 128 if offset - base + width <= 128 else 256
+
+
+def cut(value, offset):
+    moved = pltpu.roll(value, value.shape[1] - offset, 1) if offset else value
+    moved = moved[:, :128]
+    lane = lax.broadcasted_iota(jnp.int32, moved.shape, 1)
+    return jnp.where(lane < BLK, moved, 0.0)
+
+
+def kernel(
+    owner_ref, irrep_ref, occ_ref, window_ref, vir_ref,
+    slab_ref, part_ref, hole_ref, coup_ref, column_ref, row_ref, table_ref,
+    out_ref,
+    tiles, ybuf, frecv, brecv, fsend, bsend, pall_ref, hall_ref,
+    own, ystage, alphas, bases,
+    wide, left, vshift, vt, vback, amp, weight, holes, column, acc,
+    part0, part1, trip0, trip1, contrib,
+    rbuf, slots, cbuf, merged, xbuf, total, zbuf,
     ys_sem, yr_sem, hs_sem, hr_sem, ps_sem, pr_sem,
     fs_sem, fr_sem, bs_sem, br_sem, zs_sem, zr_sem, local_sem,
+    rs_sem, rr_sem, cs_sem, cr_sem, xs_sem, xr_sem, ts_sem, tr_sem,
 ):
+    half, single = jnp.bfloat16, jnp.float32
     pair, vtile, irrep, y, z = where_am_i()
+    x, core = vtile // 2, lax.rem(vtile, 2)
     zg = irrep * ZS + z
 
     def at_y(k):
@@ -48,16 +70,25 @@
         tz = lax.rem(zg + step + 2 * ZS, 2 * ZS)
         return (lax.rem(tz, ZS) * YS + y, vtile, tz // ZS)
 
+    def at_x(k):
+        tx = lax.rem(x + k, XS)
+        return tx, (pair, tx * 2 + core, irrep)
+
+    at_core = (pair, x * 2 + 1 - core, irrep)
+    at_irrep = (pair, vtile, 1 - irrep)
     barrier = pltpu.get_barrier_semaphore()
     for k in (1, 2, 3):
         pl.semaphore_signal(barrier, inc=1, device_id=at_y(k)[1], device_id_type=MESH)
+        pl.semaphore_signal(barrier, inc=1, device_id=at_x(k)[1], device_id_type=MESH)
+    pl.semaphore_signal(barrier, inc=1, device_id=at_core, device_id_type=MESH)
+    pl.semaphore_signal(barrier, inc=1, device_id=at_irrep, device_id_type=MESH)
     for step in (1, -1):
         pl.semaphore_signal(barrier, inc=1, device_id=at_z(step), device_id_type=MESH)
     for t in range(ALL - 1):
         tiles[t] = slab_ref[:, 128 * t:128 * t + 128]
     tiles[ALL - 1] = jnp.zeros((BLK, 128), jnp.bfloat16)
     tiles[ALL - 1, :, :64] = slab_ref[:, 128 * (ALL - 1):]
-    pl.semaphore_wait(barrier, 5)
+    pl.semaphore_wait(barrier, 10)
 
     def hole_copy(k):
         ty, target = at_y(k)
@@ -124,6 +155,29 @@
     own_slab.wait()
     own_part.wait()
 
+    mine_f = hall_ref[z].astype(single)
+    for source in range(YS):
+        own[80 * source:80 * source + 80, :] = mine_f[source]
+    pairs = own[pl.ds(15, YS * PER, stride=16), :]
+    lane20 = lax.broadcasted_iota(jnp.int32, (YS * PER, 128), 1).astype(single)
+    is_first, is_second = pairs[:, 16:17] == lane20, pairs[:, 17:18] == lane20
+
+    def look(mask, row):
+        return jnp.sum(jnp.where(mask, table_ref[row:row + 1, :], 0.0), axis=1, keepdims=True)
+
+    sym = look(is_first, 0).astype(jnp.int32) ^ look(is_second, 0).astype(jnp.int32)
+    energy2 = look(is_first, 1) + look(is_second, 1)
+    for w in range(NW):
+        shift = irrep_ref[window_ref[w]] ^ vtile ^ irrep
+        alphas[w] = jnp.broadcast_to(sym ^ shift, (YS * PER, 128))
+        bases[w] = jnp.broadcast_to(energy2 + occ_ref[window_ref[w]], (YS * PER, 128))
+    choose = is_second.astype(single)[:, :32].astype(half)
+    ystage[:, 24 * 30:, :] = jnp.zeros((NW, 48, 128), single)
+    for l in range(30):
+        both = jnp.dot(choose, coup_ref[l], preferred_element_type=single)
+        for w in range(NW):
+            ystage[w, 24 * l:24 * l + YS * PER, :] = both[:, 128 * w:128 * w + 128]
+
     root_y = [lax.rem(owner_ref[w], YS) for w in range(NW)]
     root_z = [owner_ref[w] // YS for w in range(NW)]
 
@@ -154,15 +208,17 @@
         def _():
             chain_copy(forward, n).wait_recv()
 
-        if forward:
-            for w in range(NW):
-                vsel_ref[n, w] = mine[w]
-
         @pl.when(jnp.logical_not(end))
         def _():
             for w in range(NW):
                 src[n, w] = jnp.where(root_z[w] == z, mine[w], dst[n, w])
             chain_copy(forward, n).start()
+
+    def hole_unit(index, p, place):
+        source = lax.rem(y + index + 1, YS)
+        lanes = pl.ds(pl.multiple_of(p * 256, 256), 256)
+        holes[place, :, lanes] = jnp.dot(
+            left[:BCH * BLK, :], weight[source, :, lanes], preferred_element_type=single)
 
     def chain_step(t, _):
         nf = t - SKEW * z
@@ -184,110 +240,52 @@
                 if step < LEFT:
                     ring_copy(RIGHT + step - 1).wait_recv()
                     ring_copy(RIGHT + step).start()
+        @pl.when(t == RING * RIGHT)
+        def _():
+            ring_copy(RIGHT - 1).wait_recv()
+            ring_copy(RIGHT + LEFT - 1).wait_recv()
+            for block in range(ZS * YS):
+                wide[80 * block:80 * block + 80, :] = hall_ref[block // YS, block % YS].astype(single)
+
+        for quarter in range(4):
+            @pl.when(t == RING * RIGHT + 1 + quarter)
+            def _():
+                for k in range(4 * quarter, 4 * quarter + 4):
+                    tile = wide[pl.ds(k, 160, stride=16), :]
+                    left[128 * k:128 * k + 128, :] = tile.T.astype(half)
+
+        @pl.when(jnp.logical_and(t >= WEIGHTS, t < WEIGHTS + YS))
+        def _():
+            source = t - WEIGHTS
+            table = wide[pl.ds(15, 160, stride=16), :]
+            slot = lax.broadcasted_iota(jnp.int32, (160, 32), 1).astype(single)
+            member = table[:, 17:18] == slot
+            for p in range(PER):
+                row = own[pl.ds(80 * source + 16 * p + 15, 1), :]
+                here = jnp.logical_and(member, table[:, 16:17] == row[:, 16:17])
+                rows = jnp.concatenate(
+                    [ystage[w, pl.ds(source * PER + p, 32, stride=24), :] for w in range(NW)], axis=1)
+                weight[source, :, 256 * p:256 * p + 256] = jnp.dot(
+                    here.astype(single).astype(half), rows.astype(half), preferred_element_type=single).astype(half)
+
+        @pl.when(jnp.logical_and(t >= HOLES, t < HOLES + 3 * PER))
+        def _():
+            hole_unit((t - HOLES) // PER, lax.rem(t - HOLES, PER), (t - HOLES) // PER)
+
         return 0
 
     lax.fori_loop(0, TILES + SKEW * (ZS - 1), chain_step, 0)
-
-    def settle(n, _):
-        for w in range(NW):
-            other = jnp.where(root_z[w] < z, frecv[n, w], brecv[n, w])
-            vsel_ref[n, w] = jnp.where(root_z[w] == z, vsel_ref[n, w], other)
-        return 0
-
-    lax.fori_loop(0, TILES, settle, 0)
 
     for k in (1, 2, 3):
         part_copy(k).wait_recv()
-    ring_copy(RIGHT - 1).wait_recv()
-    ring_copy(RIGHT + LEFT - 1).wait_recv()
-
-    def sent(n, _):
-        @pl.when(z < ZS - 1)
-        def _():
-            chain_copy(True, n).wait_send()
-
-        @pl.when(z > 0)
-        def _():
-            chain_copy(False, n).wait_send()
-
-        return 0
-
-    lax.fori_loop(0, TILES, sent, 0)
-
-    def sent_y(n, _):
-        for k in (1, 2, 3):
-            slab_copy(k, n).wait_send()
-        return 0
-
-    lax.fori_loop(0, YN, sent_y, 0)
-    for k in (1, 2, 3):
-        hole_copy(k).wait_send()
-        part_copy(k).wait_send()
-    for index in range(RIGHT + LEFT):
-        ring_copy(index).wait_send()
-
-
-def window_of(offset, width):
-    base = offset // 128 * 128
-    return base, 128 if offset - base + width <= 128 else 256
-
-
-def cut(value, offset):
-    moved = pltpu.roll(value, value.shape[1] - offset, 1) if offset else value
-    moved = moved[:, :128]
-    lane = lax.broadcasted_iota(jnp.int32, moved.shape, 1)
-    return jnp.where(lane < BLK, moved, 0.0)
-
-
-def work_kernel(
-    first_ref, second_ref, irrep_ref, occ_ref, window_ref, vir_ref,
-    hall_ref, vsel_ref, pall_ref, coup_ref, column_ref, row_ref,
-    out_ref,
-    wide, left, vshift, vt, vback, amp, weight, holes, column, acc,
-    part0, part1, trip0, trip1, contrib,
-    ybuf, slots, cbuf, merged, xbuf, total, zbuf,
-    ys_sem, yr_sem, cs_sem, cr_sem, xs_sem, xr_sem, zs_sem, zr_sem,
-):
-    half, single = jnp.bfloat16, jnp.float32
-    pair, vtile, irrep, y, z = where_am_i()
-    x, core = vtile // 2, lax.rem(vtile, 2)
-
-    def at_y(k):
-        ty = lax.rem(y + k, YS)
-        return ty, (z * YS + ty, vtile, irrep)
-
-    def at_x(k):
-        tx = lax.rem(x + k, XS)
-        return tx, (pair, tx * 2 + core, irrep)
-
-    at_core = (pair, x * 2 + 1 - core, irrep)
-    at_irrep = (pair, vtile, 1 - irrep)
-    barrier = pltpu.get_barrier_semaphore()
-    for k in (1, 2, 3):
-        pl.semaphore_signal(barrier, inc=1, device_id=at_y(k)[1], device_id_type=MESH)
-        pl.semaphore_signal(barrier, inc=1, device_id=at_x(k)[1], device_id_type=MESH)
-    pl.semaphore_signal(barrier, inc=1, device_id=at_core, device_id_type=MESH)
-    pl.semaphore_signal(barrier, inc=1, device_id=at_irrep, device_id_type=MESH)
-
-    wide[...] = hall_ref[...].astype(single)
-    for k in range(16):
-        tile = wide[pl.ds(k, 160, stride=16), :]
-        left[128 * k:128 * k + 128, :] = tile.T.astype(half)
-    table = wide[pl.ds(15, 160, stride=16), :]
-    group, member = table[:, 16:17], table[:, 17:18]
-    slot = lax.broadcasted_iota(jnp.int32, (160, 32), 1).astype(single)
-    for p in range(YS * PER):
-        here = jnp.logical_and(member == slot, group == first_ref[p].astype(single))
-        pick = here.astype(single).astype(half)
-        weight[:, 256 * p:256 * p + 256] = jnp.dot(
-            pick, coup_ref[second_ref[p]], preferred_element_type=single).astype(half)
-
     for w in range(NW):
-        for shift in range(YS):
+        for t in range(TILES):
+            other = jnp.where(root_z[w] < z, frecv[t, w], brecv[t, w])
+            vshift[:, 128 * t:128 * t + 128] = jnp.where(
+                root_z[w] == z, candidate(w, t), other).astype(single)
+        for shift in range(1, YS):
             @pl.when(y == shift)
             def _():
-                for t in range(TILES):
-                    vshift[:, 128 * t:128 * t + 128] = vsel_ref[t, w].astype(single)
                 if shift:
                     vshift[...] = pltpu.roll(vshift[...], CHL - 16 * shift, 1)
         for b in range(BCH):
@@ -304,17 +302,11 @@
             amp[w, source] = jnp.concatenate(parts, axis=0).astype(half)
     vback[:, :, BLK:] = jnp.zeros((NW, 128 * BCH, 128 - BLK), half)
     contrib[:, :, 880:PACK] = jnp.zeros((YS, BLK, PACK - 880), single)
-    pl.semaphore_wait(barrier, 8)
-
-    def alpha_of(q, w):
-        sym = irrep_ref[first_ref[q]] ^ irrep_ref[second_ref[q]]
-        return sym ^ irrep_ref[window_ref[w]] ^ vtile ^ irrep
-
     def ycopy(k):
         ty, target = at_y(k)
         return pltpu.make_async_remote_copy(
-            src_ref=contrib.at[ty], dst_ref=ybuf.at[k - 1],
-            send_sem=ys_sem.at[k - 1], recv_sem=yr_sem.at[k - 1],
+            src_ref=contrib.at[ty], dst_ref=rbuf.at[k - 1],
+            send_sem=rs_sem.at[k - 1], recv_sem=rr_sem.at[k - 1],
             device_id=target, device_id_type=MESH)
 
     gamma_row = row_ref[irrep]
@@ -322,18 +314,23 @@
     def source_step(index, _):
         source = lax.rem(y + index + 1, YS)
 
-        def hole_step(p, _):
-            lanes = pl.ds(pl.multiple_of(p * 256, 256), 256)
-            mine = pl.ds(pl.multiple_of((source * PER + p) * 256, 256), 256)
-            holes[:, lanes] = jnp.dot(left[:BCH * BLK, :], weight[:, mine], preferred_element_type=single)
-            return 0
-
-        lax.fori_loop(0, PER, hole_step, 0)
+        place = lax.rem(index, 3)
+
+        @pl.when(index == YS - 1)
+        def _():
+            def hole_step(p, _):
+                hole_unit(YS - 1, p, 0)
+                return 0
+
+            lax.fori_loop(0, PER, hole_step, 0)
+
         for w in range(NW):
             for p in range(PER):
-                q = source * PER + p
-                base = occ_ref[first_ref[q]] + occ_ref[second_ref[q]] + occ_ref[window_ref[w]]
-                column[BLK * p:BLK * p + BLK, :] = column_ref[alpha_of(q, w)] - base
+                here = pl.ds(source * PER + p, 1)
+                alpha, energy = alphas[w, here, :], column_ref[0]
+                for h in range(1, 8):
+                    energy = jnp.where(alpha == h, column_ref[h], energy)
+                column[BLK * p:BLK * p + BLK, :] = energy - bases[w, here, :]
 
             def lanes_of(t):
                 return pl.ds(pl.multiple_of(t * 256, 256), 256)
@@ -350,7 +347,7 @@
                     b = 2 * t + side
                     rows = pl.ds(pl.multiple_of(b * BLK, 8), BLK)
                     hole = jnp.concatenate([
-                        holes[rows, 256 * p + 128 * w:256 * p + 128 * w + 128] for p in range(PER)], axis=0)
+                        holes[place, rows, 256 * p + 128 * w:256 * p + 128 * w + 128] for p in range(PER)], axis=0)
                     energy = gamma_row + vir_ref[vtile, y * BCH + b]
                     inverse = pltpu.reciprocal(column[...] + energy, approx=True)
                     fill[:, 128 * side:128 * side + 128] = (
@@ -376,8 +373,8 @@
         def _():
             ty, target = at_y(index + 1)
             pltpu.make_async_remote_copy(
-                src_ref=contrib.at[ty], dst_ref=ybuf.at[index],
-                send_sem=ys_sem.at[index], recv_sem=yr_sem.at[index],
+                src_ref=contrib.at[ty], dst_ref=rbuf.at[index],
+                send_sem=rs_sem.at[index], recv_sem=rr_sem.at[index],
                 device_id=target, device_id_type=MESH).start()
 
         return 0
@@ -385,7 +382,7 @@
     lax.fori_loop(0, YS, source_step, 0)
     for k in (1, 2, 3):
         ycopy(k).wait()
-    summed = contrib[y] + ybuf[0] + ybuf[1] + ybuf[2]
+    summed = contrib[y] + rbuf[0] + rbuf[1] + rbuf[2]
     windows = [summed[:, :OUTL], pltpu.roll(summed, PACK - 440, 1)[:, :OUTL]]
     lane = lax.broadcasted_iota(jnp.int32, (1, OUTL), 1)
     codes = []
@@ -393,7 +390,8 @@
         code = jnp.full((1, OUTL), -1, jnp.int32)
         for p in range(PER):
             inside = jnp.logical_and(lane >= BLK * p, lane < BLK * (p + 1))
-            code = jnp.where(inside, alpha_of(y * PER + p, w), code)
+            alpha = jnp.concatenate([alphas[w, pl.ds(y * PER + p, 1), :]] * 4, axis=1)
+            code = jnp.where(inside, alpha, code)
         codes.append(code)
     for target in range(2 * XS):
         slots[target % 2, target // 2] = sum(
@@ -419,8 +417,32 @@
     total[...] = merged[x] + xbuf[0] + xbuf[1] + xbuf[2]
     zcopy = pltpu.make_async_remote_copy(
         src_ref=total.at[pl.ds(pl.multiple_of(40 * (1 - irrep), 8), 48), :], dst_ref=zbuf,
-        send_sem=zs_sem, recv_sem=zr_sem, device_id=at_irrep, device_id_type=MESH)
+        send_sem=ts_sem, recv_sem=tr_sem, device_id=at_irrep, device_id_type=MESH)
     zcopy.start()
+    def sent(n, _):
+        @pl.when(z < ZS - 1)
+        def _():
+            chain_copy(True, n).wait_send()
+
+        @pl.when(z > 0)
+        def _():
+            chain_copy(False, n).wait_send()
+
+        return 0
+
+    lax.fori_loop(0, TILES, sent, 0)
+
+    def sent_y(n, _):
+        for k in (1, 2, 3):
+            slab_copy(k, n).wait_send()
+        return 0
+
+    lax.fori_loop(0, YN, sent_y, 0)
+    for k in (1, 2, 3):
+        hole_copy(k).wait_send()
+        part_copy(k).wait_send()
+    for index in range(RIGHT + LEFT):
+        ring_copy(index).wait_send()
     zcopy.wait()
     out_ref[...] = total[pl.ds(pl.multiple_of(40 * irrep, 8), 48), :] + zbuf[...]
 
@@ -428,17 +450,13 @@
 DMA = pltpu.SemaphoreType.DMA
 
 
-def spread_call(owner, slab, part, hole):
-    half = jnp.bfloat16
+def call(*operands):
+    half, single = jnp.bfloat16, jnp.float32
     return pl.pallas_call(
-        spread_kernel,
-        out_shape=(
-            jax.ShapeDtypeStruct((TILES, NW, BLK, 128), half),
-            jax.ShapeDtypeStruct((YS, BLK, PACK), half),
-            jax.ShapeDtypeStruct((ZS, YS, 80, 128), half),
-        ),
-        in_specs=[SM, VM, VM, VM],
-        out_specs=(VM, VM, VM),
+        kernel,
+        out_shape=jax.ShapeDtypeStruct((48, OUTL), single),
+        in_specs=[SM] * 5 + [VM] * 7,
+        out_specs=VM,
         scratch_shapes=[
             pltpu.VMEM((ALL, BLK, 128), half),
             pltpu.VMEM((YS, TILES, BLK, 128), half),
@@ -446,30 +464,20 @@
             pltpu.VMEM((TILES, NW, BLK, 128), half),
             pltpu.VMEM((TILES, NW, BLK, 128), half),
             pltpu.VMEM((TILES, NW, BLK, 128), half),
-            DMA((3, YN)), DMA((3, YN)), DMA((3,)), DMA((3,)), DMA((3,)), DMA((3,)),
-            DMA((TILES,)), DMA((TILES,)), DMA((TILES,)), DMA((TILES,)), DMA((7,)), DMA((7,)), DMA((3,)),
-        ],
-        compiler_params=pltpu.CompilerParams(
-            collective_id=0, has_side_effects=True, vmem_limit_bytes=40 * 2**20),
-    )(owner, slab, part, hole)
-
-
-def work_call(first, second, irreps, occ, window, vir, hall, vsel, pall, coup, columns, rows):
-    half, single = jnp.bfloat16, jnp.float32
-    return pl.pallas_call(
-        work_kernel,
-        out_shape=jax.ShapeDtypeStruct((48, OUTL), single),
-        in_specs=[SM] * 6 + [VM] * 6,
-        out_specs=VM,
-        scratch_shapes=[
+            pltpu.VMEM((YS, BLK, PACK), half),
+            pltpu.VMEM((ZS, YS, 80, 128), half),
+            pltpu.VMEM((YS * 80, 128), single),
+            pltpu.VMEM((NW, 24 * 32, 128), single),
+            pltpu.VMEM((NW, YS * PER, 128), jnp.int32),
+            pltpu.VMEM((NW, YS * PER, 128), single),
             pltpu.VMEM((2560, 128), single),
             pltpu.VMEM((CHL, 160), half),
             pltpu.VMEM((BLK, CHL), single),
             pltpu.VMEM((NW, BLK, 128 * BCH), half),
             pltpu.VMEM((NW, 128 * BCH, 128), half),
             pltpu.VMEM((NW, YS, PER * BLK, 128), half),
-            pltpu.VMEM((160, 256 * YS * PER), half),
-            pltpu.VMEM((BCH * BLK, 256 * PER), single),
+            pltpu.VMEM((YS, 160, 256 * PER), half),
+            pltpu.VMEM((3, BCH * BLK, 256 * PER), single),
             pltpu.VMEM((PER * BLK, 128), single),
             pltpu.VMEM((PER * BLK, 128), single),
             pltpu.VMEM((PER * BLK, 256), single),
@@ -484,11 +492,13 @@
             pltpu.VMEM((3, BLK, OUTL), single),
             pltpu.VMEM((BLK, OUTL), single),
             pltpu.VMEM((48, OUTL), single),
+            DMA((3, YN)), DMA((3, YN)), DMA((3,)), DMA((3,)), DMA((3,)), DMA((3,)),
+            DMA((TILES,)), DMA((TILES,)), DMA((TILES,)), DMA((TILES,)), DMA((7,)), DMA((7,)), DMA((3,)),
             DMA((3,)), DMA((3,)), DMA, DMA, DMA((3,)), DMA((3,)), DMA, DMA,
         ],
         compiler_params=pltpu.CompilerParams(
-            collective_id=1, has_side_effects=True, vmem_limit_bytes=56 * 2**20),
-    )(first, second, irreps, occ, window, vir, hall, vsel, pall, coup, columns, rows)
+            collective_id=0, has_side_effects=True, vmem_limit_bytes=62 * 2**20),
+    )(*operands)
 
 
 def pick(table, index):
@@ -512,18 +522,16 @@
     hole = jnp.concatenate([send, tail], axis=2).swapaxes(0, 1).reshape(YS, PER * 16, 128)
     part = blocks[:, 1:].transpose(2, 1, 0, 3).reshape(BLK, NW * PER * BLK)
     part = jnp.pad(part, ((0, 0), (0, PACK - NW * PER * BLK)))
-    vsel, pall, hall = spread_call(owner, slabs.reshape(BLK, BLK * BLK), part, hole)
-
-    table = lax.dynamic_index_in_dim(hall, z, 0, keepdims=False).reshape(YS * PER, 16, 128)[:, 15, 16:18]
-    first, second = table[:, 0].astype(jnp.int32), table[:, 1].astype(jnp.int32)
+
     columns = jnp.broadcast_to(vir_energy[:, :, None], (8, BLK, 128))
     rows = jnp.pad(vir_energy, ((0, 0), (0, 128 - BLK)), constant_values=20.0)[:, None, :]
     keep = occ_irrep[None, :, None] ^ gamma ^ occ_irrep[None, None, :] ^ k_irrep[:, None, None]
     coup = jnp.where((keep == 0)[..., None], couplings, jnp.zeros_like(couplings))
-    coup = jnp.pad(coup, ((0, 0), (0, 2), (0, 0), (0, 128 - BLK))).transpose(2, 1, 0, 3).reshape(30, 32, 256)
-    result = work_call(
-        first, second, occ_irrep, occ_energy, window_k, vir_energy,
-        hall.reshape(2560, 128), vsel, pall, coup, columns, rows)
+    coup = jnp.pad(coup, ((0, 0), (0, 0), (0, 2), (0, 128 - BLK))).transpose(1, 2, 0, 3).reshape(30, 32, 256)
+    table = jnp.pad(jnp.stack([occ_irrep.astype(jnp.float32), occ_energy]), ((0, 6), (0, 98)))
+    result = call(
+        owner, occ_irrep, occ_energy, window_k, vir_energy,
+        slabs.reshape(BLK, BLK * BLK), part, hole, coup, columns, rows, table)
     result = lax.dynamic_slice_in_dim(result, 4 * gamma, BLK // 2, 0)[:, :PER * BLK]
     return result.reshape(BLK // 2, PER, BLK).swapaxes(0, 1).reshape(PER, 1, BLK * BLK // 2)
 

time: 141 us -> 133 us (0.943); the launches traced: 141 us -> 130 us
  Pallas kernels: 126 us -> 116 us
    pallas_call x2 -> x1, Pallas kernels: 126 us -> 116 us  [call(): pl.pallas_call(kernel, out_shape=jax.ShapeDtypeStruct((48, OUTL), single)...]
    unnamed x22 -> x14, local copies, waits for them, and re-layouts: 2.09 us -> 0.04 us
where the time goes in v3:
time: 133 us; the launch traced here: 130 us
  Pallas kernels  116 us (87%)
  local copies, waits for them, and re-layouts  9.2 us (7%)
  other arithmetic  4.49 us (3%)
    pallas_call x1, Pallas kernels, call(): pl.pallas_call(kernel, out_shape=jax.ShapeDtypeStruct((48, OUTL), single)...  116 us

profile of v3, /device:TPU:1, one launch (start us, length us, event | category | flops | bytes accessed | tf_op | source)
XLA Modules:
  0.0 130.4 jit_solution(16726031605253735635)
XLA Ops:
  0.0 1.0 select_reduce_fusion
  1.0 0.9 fusion.6
  1.8 0.1 fusion.7
  1.9 0.1 copy.31
  2.0 0.1 reshape.272
  2.1 1.4 %gather_fusion = bf16[15,7744]{1,0:T(8,128)(2,1)S(1)} fusion(bf16[5,8,7744]{2,1,0:T(8,128)(2,1)S(1)} %copy-done, s32[15]{0:T(128)S(1)} %reshape.272), kind=kCustom, calls=%fused_computation | custom fusion | bytes 464760 | tf_op jit(solution)/shard_map/jit(take_along_axis)/gather | solution.py:518
  3.5 0.0 copy-start.5
  3.5 0.0 copy-start.6
  3.5 0.5 gather.7
  4.0 0.2 copy.32
  4.2 0.1 xor_xor_fusion
  4.3 0.0 copy-start.1
  4.3 0.1 broadcast_select_fusion.1
  4.5 0.1 reshape.267
  4.7 0.1 copy.34
  4.8 0.1 fusion.2
  4.9 0.1 copy.35
  5.0 0.7 reshape.268.hole_ref
  5.7 0.1 copy.33
  5.9 0.7 pad.20.part_ref
  6.6 0.1 broadcast_xor_fusion
  6.6 0.2 xor_compare_fusion
  6.9 1.4 %broadcast_select_fusion = bf16[2,30,30,88]{3,0,2,1:T(2,128)(2,1)S(1)} fusion(bf16[2,30,30,88]{3,0,2,1:T(2,128)(2,1)S(1)} %copy-done.1, pred[2,30,30]{0,2,1:T(8,128)(4,1)S(1)} %xor_compare_fusion), kind=kLoop, calls=%fused_computation.1 | loop fusion | flops 158400 | bytes 635400 | tf_op jit(solution)/shard_map/jit(_where)/select_n | solution.py:529
  8.3 0.6 pad_bitcast_fusion
  8.8 1.1 reshape.269.coup_ref
  9.9 0.6 select_maximum_fusion.table_ref
  10.5 0.9 broadcast_in_dim.75.column_ref
  11.4 0.6 pad.23
  12.0 116.5 %shard_map.100 = f32[48,512]{1,0:T(8,128)} custom-call(s32[2]{0:T(128)} %owner_ref.1, s32[30]{0:T(128)} %irrep_ref.1, f32[30]{0:T(128)} %occ_ref.1, s32[2]{0:T(128)} %window_ref.1, f32[8,88]{1,0:T(8,128)} %vir_ref.1, bf16[88,7744]{1,0:T(8,128)(2,1)} %bitcast.31, bf16[88,896]{1,0:T(8,128)(2,1)} %pad.20.part_ref, bf16[4,80,128]{2,1,0:T(8,128)(2,1)} %reshape.268.hole_ref, ...), custom_call_target="tpu_custom_call" | custom-call | tf_op jit(solution)/shard_map/pallas_call | solution.py:455
  128.5 0.9 constant_dynamic-slice_fusion
  129.4 0.1 reshape.270
  129.6 0.8 reshape.279
  (22 shorter events, 0.1 us)
Async XLA Ops:
  0.0 2.1 %copy-start = (bf16[5,8,7744]{2,1,0:T(8,128)(2,1)S(1)}, bf16[5,8,7744]{2,1,0:T(8,128)(2,1)}, u32[]{:S(2)}) copy-start(bf16[5,8,7744]{2,1,0:T(8,128)(2,1)} %param.10) | copy-start | bytes 1858564
  3.5 1.2 copy-start.5
  3.5 1.2 copy-start.6
  4.3 2.2 %copy-start.3 = (s32[30]{0:T(128)S(1)}, s32[30]{0:T(128)}, u32[]{:S(2)}) copy-start(s32[30]{0:T(128)} %irrep_ref.1) | copy-start | bytes 364
  4.3 2.5 %copy-start.1 = (bf16[2,30,30,88]{3,0,2,1:T(2,128)(2,1)S(1)}, bf16[2,30,30,88]{3,0,2,1:T(2,128)(2,1)}, u32[]{:S(2)}) copy-start(bf16[2,30,30,88]{3,0,2,1:T(2,128)(2,1)} %param.12) | copy-start | bytes 950404
  6.9 3.1 %copy-start.4 = (f32[30]{0:T(128)S(1)}, f32[30]{0:T(128)}, u32[]{:S(2)}) copy-start(f32[30]{0:T(128)} %occ_ref.1) | copy-start | bytes 364
  6.9 3.7 %copy-start.2 = (f32[8,88]{1,0:T(8,128)S(1)}, f32[8,88]{1,0:T(8,128)}, u32[]{:S(2)}) copy-start(f32[8,88]{1,0:T(8,128)} %vir_ref.1) | copy-start | bytes 8452

commit v4 on v3

--- a/solution.py
+++ b/solution.py
@@ -46,10 +46,10 @@
 
 def kernel(
     owner_ref, irrep_ref, occ_ref, window_ref, vir_ref,
-    slab_ref, part_ref, hole_ref, coup_ref, column_ref, row_ref, table_ref,
+    slab_ref, part_ref, hole_ref, coup_ref, virs_ref,
     out_ref,
     tiles, ybuf, frecv, brecv, fsend, bsend, pall_ref, hall_ref,
-    own, ystage, alphas, bases,
+    own, ystage, alphas, bases, column_ref, square, table_ref,
     wide, left, vshift, vt, vback, amp, weight, holes, column, acc,
     part0, part1, trip0, trip1, contrib,
     rbuf, slots, cbuf, merged, xbuf, total, zbuf,
@@ -88,6 +88,19 @@
         tiles[t] = slab_ref[:, 128 * t:128 * t + 128]
     tiles[ALL - 1] = jnp.zeros((BLK, 128), jnp.bfloat16)
     tiles[ALL - 1, :, :64] = slab_ref[:, 128 * (ALL - 1):]
+    square[...] = jnp.zeros((128, 128), single)
+    square[:8, :BLK] = virs_ref[...]
+    upright = square[...].T
+    for h in range(8):
+        column_ref[h] = jnp.broadcast_to(upright[:BLK, h:h + 1], (BLK, 128))
+    lane_of = lax.broadcasted_iota(jnp.int32, (1, 128), 1)
+    irreps, energies = jnp.zeros((1, 128), jnp.int32), jnp.zeros((1, 128), single)
+    for l in range(30):
+        irreps = jnp.where(lane_of == l, irrep_ref[l], irreps)
+        energies = jnp.where(lane_of == l, occ_ref[l], energies)
+    table_ref[0:1, :] = irreps.astype(single)
+    table_ref[1:2, :] = energies
+    ystage[...] = jnp.zeros((NW, 24 * 32, 128), single)
     pl.semaphore_wait(barrier, 10)
 
     def hole_copy(k):
@@ -165,18 +178,19 @@
     def look(mask, row):
         return jnp.sum(jnp.where(mask, table_ref[row:row + 1, :], 0.0), axis=1, keepdims=True)
 
-    sym = look(is_first, 0).astype(jnp.int32) ^ look(is_second, 0).astype(jnp.int32)
+    second_irrep = look(is_second, 0).astype(jnp.int32)
+    sym = look(is_first, 0).astype(jnp.int32) ^ second_irrep
     energy2 = look(is_first, 1) + look(is_second, 1)
     for w in range(NW):
         shift = irrep_ref[window_ref[w]] ^ vtile ^ irrep
         alphas[w] = jnp.broadcast_to(sym ^ shift, (YS * PER, 128))
         bases[w] = jnp.broadcast_to(energy2 + occ_ref[window_ref[w]], (YS * PER, 128))
-    choose = is_second.astype(single)[:, :32].astype(half)
-    ystage[:, 24 * 30:, :] = jnp.zeros((NW, 48, 128), single)
-    for l in range(30):
-        both = jnp.dot(choose, coup_ref[l], preferred_element_type=single)
-        for w in range(NW):
-            ystage[w, 24 * l:24 * l + YS * PER, :] = both[:, 128 * w:128 * w + 128]
+    choose = is_second.astype(single)[:, :30].astype(half)
+    for w in range(NW):
+        wanted = second_irrep ^ irrep_ref[window_ref[w]] ^ irrep
+        for l in range(30):
+            found = jnp.dot(choose, coup_ref[w, l], preferred_element_type=single)
+            ystage[w, 24 * l:24 * l + YS * PER, :BLK] = jnp.where(wanted == irrep_ref[l], found, 0.0)
 
     root_y = [lax.rem(owner_ref[w], YS) for w in range(NW)]
     root_z = [owner_ref[w] // YS for w in range(NW)]
@@ -309,7 +323,8 @@
             send_sem=rs_sem.at[k - 1], recv_sem=rr_sem.at[k - 1],
             device_id=target, device_id_type=MESH)
 
-    gamma_row = row_ref[irrep]
+    gamma_row = square[pl.ds(irrep, 1), :]
+    gamma_row = jnp.where(lax.broadcasted_iota(jnp.int32, (1, 128), 1) < BLK, gamma_row, 20.0)
 
     def source_step(index, _):
         source = lax.rem(y + index + 1, YS)
@@ -393,32 +408,38 @@
             alpha = jnp.concatenate([alphas[w, pl.ds(y * PER + p, 1), :]] * 4, axis=1)
             code = jnp.where(inside, alpha, code)
         codes.append(code)
-    for target in range(2 * XS):
-        slots[target % 2, target // 2] = sum(
-            jnp.where(codes[w] == target, windows[w], 0.0) for w in range(NW))
-    ccopy = pltpu.make_async_remote_copy(
-        src_ref=slots.at[1 - core], dst_ref=cbuf,
-        send_sem=cs_sem, recv_sem=cr_sem, device_id=at_core, device_id_type=MESH)
-    ccopy.start()
-    ccopy.wait()
-    for tx in range(XS):
-        merged[tx] = slots[core, tx] + cbuf[tx]
-    xcopies = []
-    for k in (1, 3, 2):
-        tx, target = at_x(k)
-        xcopies.append(pltpu.make_async_remote_copy(
-            src_ref=merged.at[tx], dst_ref=xbuf.at[k - 1],
-            send_sem=xs_sem.at[k - 1], recv_sem=xr_sem.at[k - 1],
-            device_id=target, device_id_type=MESH))
-    for copy in xcopies:
-        copy.start()
-    for copy in xcopies:
-        copy.wait()
-    total[...] = merged[x] + xbuf[0] + xbuf[1] + xbuf[2]
-    zcopy = pltpu.make_async_remote_copy(
-        src_ref=total.at[pl.ds(pl.multiple_of(40 * (1 - irrep), 8), 48), :], dst_ref=zbuf,
-        send_sem=ts_sem, recv_sem=tr_sem, device_id=at_irrep, device_id_type=MESH)
-    zcopy.start()
+    ccopies, xcopies, zcopies = [], [], []
+    for part in range(2):
+        lanes = slice(256 * part, 256 * part + 256)
+        for target in range(2 * XS):
+            slots[part, target % 2, target // 2] = sum(
+                jnp.where(codes[w][:, lanes] == target, windows[w][:, lanes], 0.0) for w in range(NW))
+        ccopies.append(pltpu.make_async_remote_copy(
+            src_ref=slots.at[part, 1 - core], dst_ref=cbuf.at[part],
+            send_sem=cs_sem.at[part], recv_sem=cr_sem.at[part], device_id=at_core, device_id_type=MESH))
+        ccopies[part].start()
+    for part in range(2):
+        ccopies[part].wait()
+        for tx in range(XS):
+            merged[part, tx] = slots[part, core, tx] + cbuf[part, tx]
+        sends = []
+        for k in (1, 3, 2):
+            tx, target = at_x(k)
+            sends.append(pltpu.make_async_remote_copy(
+                src_ref=merged.at[part, tx], dst_ref=xbuf.at[part, k - 1],
+                send_sem=xs_sem.at[part, k - 1], recv_sem=xr_sem.at[part, k - 1],
+                device_id=target, device_id_type=MESH))
+        for copy in sends:
+            copy.start()
+        xcopies.append(sends)
+    for part in range(2):
+        for copy in xcopies[part]:
+            copy.wait()
+        total[part] = merged[part, x] + xbuf[part, 0] + xbuf[part, 1] + xbuf[part, 2]
+        zcopies.append(pltpu.make_async_remote_copy(
+            src_ref=total.at[part, pl.ds(pl.multiple_of(40 * (1 - irrep), 8), 48), :], dst_ref=zbuf.at[part],
+            send_sem=ts_sem.at[part], recv_sem=tr_sem.at[part], device_id=at_irrep, device_id_type=MESH))
+        zcopies[part].start()
     def sent(n, _):
         @pl.when(z < ZS - 1)
         def _():
@@ -443,8 +464,10 @@
         part_copy(k).wait_send()
     for index in range(RIGHT + LEFT):
         ring_copy(index).wait_send()
-    zcopy.wait()
-    out_ref[...] = total[pl.ds(pl.multiple_of(40 * irrep, 8), 48), :] + zbuf[...]
+    for part in range(2):
+        zcopies[part].wait()
+        out_ref[:, 256 * part:256 * part + 256] = (
+            total[part, pl.ds(pl.multiple_of(40 * irrep, 8), 48), :] + zbuf[part])
 
 
 DMA = pltpu.SemaphoreType.DMA
@@ -455,7 +478,7 @@
     return pl.pallas_call(
         kernel,
         out_shape=jax.ShapeDtypeStruct((48, OUTL), single),
-        in_specs=[SM] * 5 + [VM] * 7,
+        in_specs=[SM] * 5 + [VM] * 5,
         out_specs=VM,
         scratch_shapes=[
             pltpu.VMEM((ALL, BLK, 128), half),
@@ -470,6 +493,9 @@
             pltpu.VMEM((NW, 24 * 32, 128), single),
             pltpu.VMEM((NW, YS * PER, 128), jnp.int32),
             pltpu.VMEM((NW, YS * PER, 128), single),
+            pltpu.VMEM((8, BLK, 128), single),
+            pltpu.VMEM((128, 128), single),
+            pltpu.VMEM((8, 128), single),
             pltpu.VMEM((2560, 128), single),
             pltpu.VMEM((CHL, 160), half),
             pltpu.VMEM((BLK, CHL), single),
@@ -486,15 +512,15 @@
             pltpu.VMEM((PER * BLK, 256), half),
             pltpu.VMEM((YS, BLK, PACK), single),
             pltpu.VMEM((3, BLK, PACK), single),
-            pltpu.VMEM((2, XS, BLK, OUTL), single),
-            pltpu.VMEM((XS, BLK, OUTL), single),
-            pltpu.VMEM((XS, BLK, OUTL), single),
-            pltpu.VMEM((3, BLK, OUTL), single),
-            pltpu.VMEM((BLK, OUTL), single),
-            pltpu.VMEM((48, OUTL), single),
+            pltpu.VMEM((2, 2, XS, BLK, 256), single),
+            pltpu.VMEM((2, XS, BLK, 256), single),
+            pltpu.VMEM((2, XS, BLK, 256), single),
+            pltpu.VMEM((2, 3, BLK, 256), single),
+            pltpu.VMEM((2, BLK, 256), single),
+            pltpu.VMEM((2, 48, 256), single),
             DMA((3, YN)), DMA((3, YN)), DMA((3,)), DMA((3,)), DMA((3,)), DMA((3,)),
             DMA((TILES,)), DMA((TILES,)), DMA((TILES,)), DMA((TILES,)), DMA((7,)), DMA((7,)), DMA((3,)),
-            DMA((3,)), DMA((3,)), DMA, DMA, DMA((3,)), DMA((3,)), DMA, DMA,
+            DMA((3,)), DMA((3,)), DMA((2,)), DMA((2,)), DMA((2, 3)), DMA((2, 3)), DMA((2,)), DMA((2,)),
         ],
         compiler_params=pltpu.CompilerParams(
             collective_id=0, has_side_effects=True, vmem_limit_bytes=62 * 2**20),
@@ -523,15 +549,9 @@
     part = blocks[:, 1:].transpose(2, 1, 0, 3).reshape(BLK, NW * PER * BLK)
     part = jnp.pad(part, ((0, 0), (0, PACK - NW * PER * BLK)))
 
-    columns = jnp.broadcast_to(vir_energy[:, :, None], (8, BLK, 128))
-    rows = jnp.pad(vir_energy, ((0, 0), (0, 128 - BLK)), constant_values=20.0)[:, None, :]
-    keep = occ_irrep[None, :, None] ^ gamma ^ occ_irrep[None, None, :] ^ k_irrep[:, None, None]
-    coup = jnp.where((keep == 0)[..., None], couplings, jnp.zeros_like(couplings))
-    coup = jnp.pad(coup, ((0, 0), (0, 0), (0, 2), (0, 128 - BLK))).transpose(1, 2, 0, 3).reshape(30, 32, 256)
-    table = jnp.pad(jnp.stack([occ_irrep.astype(jnp.float32), occ_energy]), ((0, 6), (0, 98)))
     result = call(
         owner, occ_irrep, occ_energy, window_k, vir_energy,
-        slabs.reshape(BLK, BLK * BLK), part, hole, coup, columns, rows, table)
+        slabs.reshape(BLK, BLK * BLK), part, hole, couplings, vir_energy)
     result = lax.dynamic_slice_in_dim(result, 4 * gamma, BLK // 2, 0)[:, :PER * BLK]
     return result.reshape(BLK // 2, PER, BLK).swapaxes(0, 1).reshape(PER, 1, BLK * BLK // 2)
 

time: 133 us -> 124 us (0.932)
  the two profiles are of different devices: /device:TPU:1 before, /device:TPU:8 now
where the time goes in v4:
time: 124 us
  Pallas kernels  114 us (92%)
  local copies, waits for them, and re-layouts  6.85 us (6%)
  other arithmetic  2.92 us (2%)
    pallas_call x1, Pallas kernels, call(): pl.pallas_call(kernel, out_shape=jax.ShapeDtypeStruct((48, OUTL), single)...  114 us

profile of v4, /device:TPU:8, one launch (start us, length us, event | category | flops | bytes accessed | tf_op | source)
XLA Modules:
  0.0 123.8 jit_solution(8938033624482383061)
XLA Ops:
  0.0 0.0 copy-start
  0.0 0.9 fusion.6
  0.9 0.7 convert_bitcast_fusion
  1.6 0.9 select_reduce_fusion
  2.5 0.1 fusion.7
  2.6 0.1 xor_xor_fusion
  2.7 0.1 copy.37
  2.8 0.1 copy.34
  2.9 0.1 reshape.231
  3.0 0.0 copy-done
  3.0 1.4 %gather_fusion = bf16[15,7744]{1,0:T(8,128)(2,1)S(1)} fusion(bf16[5,8,7744]{2,1,0:T(8,128)(2,1)S(1)} %copy-done, s32[15]{0:T(128)S(1)} %reshape.231), kind=kCustom, calls=%fused_computation | custom fusion | bytes 464760 | tf_op jit(solution)/shard_map/jit(take_along_axis)/gather | solution.py:544
  4.4 0.5 gather.7
  4.9 0.2 copy.35
  5.1 0.0 copy-start.1
  5.1 0.1 broadcast_select_fusion
  5.3 0.1 reshape.227
  5.4 0.1 fusion.2
  5.5 0.2 copy.36
  5.7 0.7 pad.8.part_ref
  6.4 0.1 copy.38
  6.4 0.7 reshape.228.hole_ref
  7.1 0.0 copy-done.1
  7.2 0.8 copy.39.coup_ref
  8.0 113.9 %shard_map.100 = f32[48,512]{1,0:T(8,128)} custom-call(s32[2]{0:T(128)} %owner_ref.1, s32[30]{0:T(128)} %irrep_ref.1, f32[30]{0:T(128)} %occ_ref.1, s32[2]{0:T(128)} %window_ref.1, f32[8,88]{1,0:T(8,128)} %virs_ref.1, bf16[88,7744]{1,0:T(8,128)(2,1)} %bitcast.25, bf16[88,896]{1,0:T(8,128)(2,1)} %pad.8.part_ref, bf16[4,80,128]{2,1,0:T(8,128)(2,1)} %reshape.228.hole_ref, ...), custom_call_target="tpu_custom_call" | custom-call | tf_op jit(solution)/shard_map/pallas_call | solution.py:478
  121.9 0.9 constant_dynamic-slice_fusion
  122.8 0.1 reshape.229
  123.0 0.8 reshape.238
  (9 shorter events, 0.1 us)
Async XLA Ops:
  0.0 3.0 %copy-start = (bf16[5,8,7744]{2,1,0:T(8,128)(2,1)S(1)}, bf16[5,8,7744]{2,1,0:T(8,128)(2,1)}, u32[]{:S(2)}) copy-start(bf16[5,8,7744]{2,1,0:T(8,128)(2,1)} %param.10) | copy-start | bytes 1858564
  5.1 2.1 %copy-start.1 = (bf16[2,30,30,88]{3,0,2,1:T(2,128)(2,1)S(1)}, bf16[2,30,30,88]{3,0,2,1:T(2,128)(2,1)}, u32[]{:S(2)}) copy-start(bf16[2,30,30,88]{3,0,2,1:T(2,128)(2,1)} %param.12) | copy-start | bytes 950404

commit v5 on v4

--- a/solution.py
+++ b/solution.py
@@ -18,8 +18,7 @@
 YN = TILES // YPER
 SKEW = 4
 RING = 4
-WEIGHTS = RING * 4 + 5
-HOLES = WEIGHTS + 4
+UNITS = 24
 RIGHT, LEFT = 4, 3
 PACK = 896
 OUTL = 512
@@ -234,6 +233,8 @@
         holes[place, :, lanes] = jnp.dot(
             left[:BCH * BLK, :], weight[source, :, lanes], preferred_element_type=single)
 
+    begin = RING * RIGHT + 5 * jnp.minimum(z, ZS - 1 - z)
+
     def chain_step(t, _):
         nf = t - SKEW * z
         nb = t - SKEW * (ZS - 1 - z)
@@ -254,7 +255,7 @@
                 if step < LEFT:
                     ring_copy(RIGHT + step - 1).wait_recv()
                     ring_copy(RIGHT + step).start()
-        @pl.when(t == RING * RIGHT)
+        @pl.when(t == begin)
         def _():
             ring_copy(RIGHT - 1).wait_recv()
             ring_copy(RIGHT + LEFT - 1).wait_recv()
@@ -262,15 +263,15 @@
                 wide[80 * block:80 * block + 80, :] = hall_ref[block // YS, block % YS].astype(single)
 
         for quarter in range(4):
-            @pl.when(t == RING * RIGHT + 1 + quarter)
+            @pl.when(t == begin + 1 + quarter)
             def _():
                 for k in range(4 * quarter, 4 * quarter + 4):
                     tile = wide[pl.ds(k, 160, stride=16), :]
                     left[128 * k:128 * k + 128, :] = tile.T.astype(half)
 
-        @pl.when(jnp.logical_and(t >= WEIGHTS, t < WEIGHTS + YS))
-        def _():
-            source = t - WEIGHTS
+        @pl.when(jnp.logical_and(t >= (begin + 5), t < (begin + 5) + YS))
+        def _():
+            source = t - (begin + 5)
             table = wide[pl.ds(15, 160, stride=16), :]
             slot = lax.broadcasted_iota(jnp.int32, (160, 32), 1).astype(single)
             member = table[:, 17:18] == slot
@@ -282,13 +283,13 @@
                 weight[source, :, 256 * p:256 * p + 256] = jnp.dot(
                     here.astype(single).astype(half), rows.astype(half), preferred_element_type=single).astype(half)
 
-        @pl.when(jnp.logical_and(t >= HOLES, t < HOLES + 3 * PER))
-        def _():
-            hole_unit((t - HOLES) // PER, lax.rem(t - HOLES, PER), (t - HOLES) // PER)
+        @pl.when(jnp.logical_and(t >= (begin + 9), t < (begin + 9) + 3 * PER))
+        def _():
+            hole_unit((t - (begin + 9)) // PER, lax.rem(t - (begin + 9), PER), (t - (begin + 9)) // PER)
 
         return 0
 
-    lax.fori_loop(0, TILES + SKEW * (ZS - 1), chain_step, 0)
+    lax.fori_loop(0, RING * RIGHT + 15 + UNITS + 1, chain_step, 0)
 
     for k in (1, 2, 3):
         part_copy(k).wait_recv()

time: 124 us -> 126 us (1.016)
  the two profiles are of different devices: /device:TPU:8 before, /device:TPU:57 now
where the time goes in v5:
time: 126 us; the launch traced here: 125 us
  Pallas kernels  116 us (92%)
  local copies, waits for them, and re-layouts  6.85 us (5%)
  other arithmetic  2.92 us (2%)
    pallas_call x1, Pallas kernels, call(): pl.pallas_call(kernel, out_shape=jax.ShapeDtypeStruct((48, OUTL), single)...  116 us

profile of v5, /device:TPU:57, one launch (start us, length us, event | category | flops | bytes accessed | tf_op | source)
XLA Modules:
  0.0 125.4 jit_solution(163032894386752984)
XLA Ops:
  0.0 0.0 copy-start
  0.0 0.9 fusion.6
  0.9 0.7 convert_bitcast_fusion
  1.6 0.9 select_reduce_fusion
  2.5 0.1 fusion.7
  2.6 0.1 xor_xor_fusion
  2.7 0.1 copy.37
  2.8 0.1 copy.34
  2.9 0.1 reshape.231
  3.0 0.0 copy-done
  3.0 1.4 %gather_fusion = bf16[15,7744]{1,0:T(8,128)(2,1)S(1)} fusion(bf16[5,8,7744]{2,1,0:T(8,128)(2,1)S(1)} %copy-done, s32[15]{0:T(128)S(1)} %reshape.231), kind=kCustom, calls=%fused_computation | custom fusion | bytes 464760 | tf_op jit(solution)/shard_map/jit(take_along_axis)/gather | solution.py:545
  4.4 0.5 gather.7
  4.9 0.2 copy.35
  5.1 0.0 copy-start.1
  5.1 0.1 broadcast_select_fusion
  5.3 0.1 reshape.227
  5.4 0.1 fusion.2
  5.5 0.2 copy.36
  5.7 0.7 pad.8.part_ref
  6.4 0.1 copy.38
  6.4 0.7 reshape.228.hole_ref
  7.1 0.0 copy-done.1
  7.2 0.8 copy.39.coup_ref
  8.0 115.6 %shard_map.100 = f32[48,512]{1,0:T(8,128)} custom-call(s32[2]{0:T(128)} %owner_ref.1, s32[30]{0:T(128)} %irrep_ref.1, f32[30]{0:T(128)} %occ_ref.1, s32[2]{0:T(128)} %window_ref.1, f32[8,88]{1,0:T(8,128)} %virs_ref.1, bf16[88,7744]{1,0:T(8,128)(2,1)} %bitcast.25, bf16[88,896]{1,0:T(8,128)(2,1)} %pad.8.part_ref, bf16[4,80,128]{2,1,0:T(8,128)(2,1)} %reshape.228.hole_ref, ...), custom_call_target="tpu_custom_call" | custom-call | tf_op jit(solution)/shard_map/pallas_call | solution.py:479
  123.6 0.9 constant_dynamic-slice_fusion
  124.5 0.1 reshape.229
  124.6 0.8 reshape.238
  (9 shorter events, 0.1 us)
Async XLA Ops:
  0.0 3.0 %copy-start = (bf16[5,8,7744]{2,1,0:T(8,128)(2,1)S(1)}, bf16[5,8,7744]{2,1,0:T(8,128)(2,1)}, u32[]{:S(2)}) copy-start(bf16[5,8,7744]{2,1,0:T(8,128)(2,1)} %param.10) | copy-start | bytes 1858564
  5.1 2.1 %copy-start.1 = (bf16[2,30,30,88]{3,0,2,1:T(2,128)(2,1)S(1)}, bf16[2,30,30,88]{3,0,2,1:T(2,128)(2,1)}, u32[]{:S(2)}) copy-start(bf16[2,30,30,88]{3,0,2,1:T(2,128)(2,1)} %param.12) | copy-start | bytes 950404
